TPU v7x, 256 devices: a whole 4x4x8 slice. The times are simulated.
256 devices in a mesh: dp: 4 (over z_hi, core), ctx: 16 (over x, z_lo), tensor: 4 (over y).
Axes of the slice: x: 4, y: 4, z: 8 (z_hi: 2, z_lo: 4; z = z_hi * 4 + z_lo), core: 2. Of those that a mesh axis runs over, the one named last changes fastest.
Arguments:
- hidden_states: bfloat16 [4, 2048, 8192], P('dp', 'ctx'), may hold values from -6 to 6
- positions: int32 [4, 2048], P('dp', 'ctx'), may hold values from 0 to 2047, as said below
- queries: bfloat16 [4, 2048, 4096], P('dp', 'ctx', 'tensor'), may hold values from -32 to 32
- key_weight: bfloat16 [8192, 512], P('ctx', 'tensor'), may hold values from -0.06641333 to 0.06641333
- value_weight: bfloat16 [8192, 512], P('ctx', 'tensor'), may hold values from -0.0625 to 0.0625
- key_step: float32 [64, 512], P('ctx', 'tensor'), may hold values from 0.003 to 0.01
- value_step: float32 [64, 512], P('ctx', 'tensor'), may hold values from 0.003 to 0.01
- smoothing: float32 [8192], replicated, may hold values from 0.5 to 2
- grad_out: bfloat16 [4, 2048, 4096], P('dp', 'ctx', 'tensor'), may hold values from -6 to 6
Outputs:
- grad_hidden: float32 [4, 2048, 8192], P('dp', 'ctx', 'tensor')
- grad_queries: float32 [4, 2048, 4096], P('dp', 'ctx', 'tensor')
- grad_key_weight: float32 [8192, 512], P('ctx', 'tensor')
- grad_value_weight: float32 [8192, 512], P('ctx', 'tensor')
- grad_key_step: float32 [64, 512], P('ctx', 'tensor')
- grad_value_step: float32 [64, 512], P('ctx', 'tensor')
- grad_smoothing: float32 [8192], replicated
Inputs may be any that keep to these rules, and one draw needn't show every extreme that they name: In each sequence positions start at 0 and rise by one from token to token, returning to 0 at the start of each of at most three documents; the first sequence is a single document.
All inputs are finite; a program needn't handle non-finite values.
Results may differ from a plain program's by a relative error of at most 0.029.
The roundings to bfloat16 on the way count: a program that leaves them out, or rounds other values in their place, can miss the bound.
Values may be sent and summed in bfloat16 or wider, within the bound.
A program may use at most 64 MiB of HBM per device.

v0:
```python
import math

import jax
import jax.numpy as jnp
from jax import lax
from jax.sharding import PartitionSpec as P

HD = 128
GROUP = 128


TWO_PI = 2.0 * math.pi
NEG_FILL = -1e30


def rope_tables(positions):
    half_size = HD // 2
    frequency = jnp.exp(jnp.arange(half_size, dtype=jnp.float32) * (-2.0 * math.log(10000.0) / HD))
    angles = positions.astype(jnp.float32)[..., None] * frequency
    return (jnp.cos(angles), jnp.sin(angles))


def rotate(vectors, cosine, sine_part):
    half_size = vectors.shape[-1] // 2
    lower_half = vectors[..., :half_size]
    upper_half = vectors[..., half_size:]
    return jnp.concatenate(
        [
            lower_half * cosine - upper_half * sine_part,
            upper_half * cosine + lower_half * sine_part,
        ],
        axis=-1,
    )


def unrotate(gradient, cosine, sine_part):
    half_size = gradient.shape[-1] // 2
    lower_half = gradient[..., :half_size]
    upper_half = gradient[..., half_size:]
    return jnp.concatenate(
        [
            lower_half * cosine + upper_half * sine_part,
            upper_half * cosine - lower_half * sine_part,
        ],
        axis=-1,
    )


def quantize(weight, step_size, smooth_vec):
    step_rows = jnp.repeat(step_size, GROUP, axis=0)
    code_ratio = weight.astype(jnp.float32) * smooth_vec[:, None] / step_rows
    soft_level = code_ratio - jnp.sin(TWO_PI * code_ratio) / TWO_PI
    return ((step_rows * soft_level).astype(jnp.bfloat16), code_ratio)


def weight_terms(gradient, code_ratio, slope_term, smooth_vec):
    phase_angle = TWO_PI * code_ratio
    grad_weight = gradient * slope_term * smooth_vec[:, None]
    per_entry = gradient * (code_ratio * jnp.cos(phase_angle) - jnp.sin(phase_angle) / TWO_PI)
    grad_step = per_entry.reshape(-1, GROUP, per_entry.shape[1]).sum(axis=1)
    return (grad_weight, grad_step)


def body(
    hidden_states,
    positions,
    queries,
    key_weight,
    value_weight,
    key_step,
    value_step,
    smoothing,
    grad_out,
):
    tok_rows = hidden_states.shape[1]
    width = hidden_states.shape[2]
    group_q = queries.shape[2] // HD
    shard_index = lax.axis_index("ctx")
    length = tok_rows * lax.axis_size("ctx")
    shard_rows = key_weight.shape[0]
    block_rows = min(512, length)
    score_scale = HD ** (-0.5)
    smoothed = (hidden_states[0].astype(jnp.float32) / smoothing).astype(jnp.bfloat16)
    smooth_rows = lax.dynamic_slice_in_dim(smoothing, shard_index * shard_rows, shard_rows)
    key_part, ratio_key = quantize(key_weight, key_step, smooth_rows)
    value_part, ratio_value = quantize(value_weight, value_step, smooth_rows)
    key_full, value_full = (
        lax.all_gather(key_part, "ctx", axis=0, tiled=True),
        lax.all_gather(value_part, "ctx", axis=0, tiled=True),
    )
    key_raw = jnp.dot(smoothed, key_full, preferred_element_type=jnp.float32)
    values = jnp.dot(smoothed, value_full, preferred_element_type=jnp.float32).astype(jnp.bfloat16)
    position = positions[0]
    cosine, sine_part = rope_tables(position)
    keys = rotate(key_raw, cosine, sine_part).astype(jnp.bfloat16)
    q_rot = rotate(
        queries[0].astype(jnp.float32).reshape(tok_rows, group_q, HD),
        cosine[:, None, :],
        sine_part[:, None, :],
    ).astype(jnp.bfloat16)
    q_index = shard_index * tok_rows + jnp.arange(tok_rows, dtype=jnp.int32)
    offset = position - q_index
    keys_all, values_all, offset_all = (
        lax.all_gather(keys, "ctx", axis=0, tiled=True),
        lax.all_gather(values, "ctx", axis=0, tiled=True),
        lax.all_gather(offset, "ctx", axis=0, tiled=True),
    )
    block_count = ((shard_index + 1) * tok_rows + block_rows - 1) // block_rows

    def scores_of(row_start):
        key_block = lax.dynamic_slice_in_dim(keys_all, row_start, block_rows)
        offset_block = lax.dynamic_slice_in_dim(offset_all, row_start, block_rows)
        key_order = row_start + jnp.arange(block_rows, dtype=jnp.int32)
        allowed = (key_order[None, :] <= q_index[:, None]) & (
            offset_block[None, :] == offset[:, None]
        )
        raw_scores = (
            jnp.einsum("qgd,kd->gqk", q_rot, key_block, preferred_element_type=jnp.float32)
            * score_scale
        )
        return (raw_scores, allowed[None], key_block)

    def stats_step(block_num, state_pair):
        running_max, running_sum = state_pair
        raw_scores, allowed, unused_keys = scores_of(block_num * block_rows)
        masked = jnp.where(allowed, raw_scores, NEG_FILL)
        new_max = jnp.maximum(running_max, jnp.max(masked, axis=2))
        block_sum = jnp.sum(jnp.where(allowed, jnp.exp(masked - new_max[..., None]), 0.0), axis=2)
        return (new_max, running_sum * jnp.exp(running_max - new_max) + block_sum)

    start_pair = (
        jnp.full((group_q, tok_rows), NEG_FILL, jnp.float32),
        jnp.zeros((group_q, tok_rows), jnp.float32),
    )
    running_max, running_sum = lax.fori_loop(0, block_count, stats_step, start_pair)

    def probs_of(row_start):
        raw_scores, allowed, key_block = scores_of(row_start)
        soft_weights = (
            jnp.where(allowed, jnp.exp(raw_scores - running_max[..., None]), 0.0)
            / running_sum[..., None]
        )
        value_block = lax.dynamic_slice_in_dim(values_all, row_start, block_rows)
        return (soft_weights, key_block, value_block)

    def output_step(block_num, accumulated):
        soft_weights, unused_keys, value_block = probs_of(block_num * block_rows)
        return accumulated + jnp.einsum(
            "gqk,kd->qgd",
            soft_weights.astype(jnp.bfloat16),
            value_block,
            preferred_element_type=jnp.float32,
        )

    attended = lax.fori_loop(
        0, block_count, output_step, jnp.zeros((tok_rows, group_q, HD), jnp.float32)
    )
    dout_rows = grad_out[0].reshape(tok_rows, group_q, HD)
    delta_rows = jnp.sum(dout_rows.astype(jnp.float32) * attended, axis=2).T

    def grad_step(block_num, state_triple):
        query_acc, key_acc, value_acc = state_triple
        row_start = block_num * block_rows
        soft_weights, key_block, value_block = probs_of(row_start)
        d_probs = jnp.einsum(
            "qgd,kd->gqk", dout_rows, value_block, preferred_element_type=jnp.float32
        )
        d_scores = (soft_weights * (d_probs - delta_rows[..., None])).astype(jnp.bfloat16)
        query_acc = query_acc + jnp.einsum(
            "gqk,kd->qgd", d_scores, key_block, preferred_element_type=jnp.float32
        )
        key_block_grad = (
            jnp.einsum("gqk,qgd->kd", d_scores, q_rot, preferred_element_type=jnp.float32)
            * score_scale
        )
        value_block_grad = jnp.einsum(
            "gqk,qgd->kd",
            soft_weights.astype(jnp.bfloat16),
            dout_rows,
            preferred_element_type=jnp.float32,
        )
        key_acc = lax.dynamic_update_slice_in_dim(key_acc, key_block_grad, row_start, 0)
        value_acc = lax.dynamic_update_slice_in_dim(value_acc, value_block_grad, row_start, 0)
        return (query_acc, key_acc, value_acc)

    start_triple = (
        jnp.zeros((tok_rows, group_q, HD), jnp.float32),
        jnp.zeros((length, HD), jnp.float32),
        jnp.zeros((length, HD), jnp.float32),
    )
    query_acc, key_acc, value_acc = lax.fori_loop(0, block_count, grad_step, start_triple)
    key_local, value_local = (
        lax.psum_scatter(key_acc, "ctx", scatter_dimension=0, tiled=True),
        lax.psum_scatter(value_acc, "ctx", scatter_dimension=0, tiled=True),
    )
    grad_queries = unrotate(
        query_acc * score_scale, cosine[:, None, :], sine_part[:, None, :]
    ).reshape(1, tok_rows, group_q * HD)
    key_rounded = unrotate(key_local, cosine, sine_part).astype(jnp.bfloat16)
    value_rounded = value_local.astype(jnp.bfloat16)
    d_smoothed = jnp.einsum(
        "th,dh->td", key_rounded, key_full, preferred_element_type=jnp.float32
    ) + jnp.einsum("th,dh->td", value_rounded, value_full, preferred_element_type=jnp.float32)
    d_columns = lax.psum_scatter(d_smoothed, "tensor", scatter_dimension=1, tiled=True)
    part_width = d_columns.shape[1]
    column_start = lax.axis_index("tensor") * part_width
    smooth_cols = lax.dynamic_slice_in_dim(smoothing, column_start, part_width)
    hidden_cols = lax.dynamic_slice_in_dim(hidden_states[0], column_start, part_width, 1).astype(
        jnp.float32
    )
    grad_hidden = (d_columns / smooth_cols)[None]
    active_term = -jnp.sum(d_columns * hidden_cols, axis=0) / (smooth_cols * smooth_cols)
    both_grads = jnp.concatenate([key_rounded, value_rounded], axis=1)
    weight_grads = lax.psum_scatter(
        jnp.einsum("td,th->dh", smoothed, both_grads, preferred_element_type=jnp.float32),
        "ctx",
        scatter_dimension=0,
        tiled=True,
    )
    slope_key = 1.0 - jnp.cos(TWO_PI * ratio_key)
    slope_value = 1.0 - jnp.cos(TWO_PI * ratio_value)
    head_width = key_weight.shape[1]
    smooth_local = jnp.sum(
        weight_grads[:, :head_width] * slope_key * key_weight.astype(jnp.float32), axis=1
    )
    smooth_local = smooth_local + jnp.sum(
        weight_grads[:, head_width:] * slope_value * value_weight.astype(jnp.float32), axis=1
    )
    smooth_term = lax.dynamic_update_slice_in_dim(
        jnp.zeros((width,), jnp.float32), smooth_local, shard_index * shard_rows, 0
    )
    smooth_term = smooth_term + lax.dynamic_update_slice_in_dim(
        jnp.zeros((width,), jnp.float32), active_term, column_start, 0
    )
    weight_grads = lax.psum(weight_grads, "dp")
    grad_smoothing = lax.psum(smooth_term, ("dp", "ctx", "tensor"))
    key_wgrad, key_sgrad = weight_terms(
        weight_grads[:, :head_width], ratio_key, slope_key, smooth_rows
    )
    value_wgrad, value_sgrad = weight_terms(
        weight_grads[:, head_width:], ratio_value, slope_value, smooth_rows
    )
    return (
        grad_hidden,
        grad_queries,
        key_wgrad,
        value_wgrad,
        key_sgrad,
        value_sgrad,
        grad_smoothing,
    )


def solution(mesh):
    in_specs = (
        P("dp", "ctx", None),
        P("dp", "ctx"),
        P("dp", "ctx", "tensor"),
        P("ctx", "tensor"),
        P("ctx", "tensor"),
        P("ctx", "tensor"),
        P("ctx", "tensor"),
        P(),
        P("dp", "ctx", "tensor"),
    )
    out_specs = (
        P("dp", "ctx", "tensor"),
        P("dp", "ctx", "tensor"),
        P("ctx", "tensor"),
        P("ctx", "tensor"),
        P("ctx", "tensor"),
        P("ctx", "tensor"),
        P(),
    )
    return jax.shard_map(body, mesh=mesh, in_specs=in_specs, out_specs=out_specs, check_vma=False)
```

profile of v0, /device:TPU:1, one launch (start us, length us, event | category | flops | bytes accessed | tf_op | source)
XLA Modules:
  0.0 841.1 jit_solution(13145893839699127626)
XLA Ops:
  7.2 0.8 dynamic_slice.33
  8.0 3.6 fusion.56
  11.7 0.7 all-gather.6.cloned.1.call-update
  12.5 0.7 bitcast_convert_fusion
  13.1 2.1 fusion.51
  15.2 38.5 %all-gather = s32[16,1,128]{2,1,0:T(1,128)S(1)} all-gather(s32[1,1,128]{2,1,0:T(1,128)S(1)} %get-tuple-element.484), channel_id=1, replica_groups=mesh['dp'=4,'ctx'=16,'tensor'=4] {'ctx'}, dimensions={0}, use_global_device_ids=true | all-gather | bytes 8704 | tf_op jit(solution)/shard_map/all_gather | solution.py:106
  54.3 39.3 %all-gather.4.cloned.1.call-done = bf16[8192,128]{1,0:T(8,128)(2,1)} async-done(((bf16[512,128]{1,0:T(8,128)(2,1)}), bf16[8192,128]{1,0:T(8,128)(2,1)}) %all-gather.4.cloned.1.call-update) | async-done | bytes 2097168 | tf_op jit(solution)/shard_map/all_gather | solution.py:88
  93.6 2.5 fusion.86
  96.3 44.3 %all_gather.16 = bf16[2048,128]{0,1:T(8,128)(2,1)} all-gather(bf16[128,128]{0,1:T(8,128)(2,1)S(1)} %pad_maximum_fusion.2), channel_id=1, replica_groups=mesh['dp'=4,'ctx'=16,'tensor'=4] {'ctx'}, dimensions={0}, use_global_device_ids=true | all-gather | bytes 557056 | tf_op jit(solution)/shard_map/all_gather | solution.py:104
  140.7 2.0 copy.57
  143.0 2.3 while.39
  143.4 1.4 fusion.125
  144.7 0.5 select_reduce_fusion.2
  145.3 39.9 %all-gather.6.cloned.1.call-done = bf16[8192,128]{1,0:T(8,128)(2,1)} async-done(((bf16[512,128]{1,0:T(8,128)(2,1)}), bf16[8192,128]{1,0:T(8,128)(2,1)}) %all-gather.6.cloned.1.call-update) | async-done | bytes 2097168 | tf_op jit(solution)/shard_map/all_gather | solution.py:89
  185.2 2.3 convolution_convert_fusion
  187.5 39.2 %all_gather.19 = bf16[2048,128]{1,0:T(8,128)(2,1)S(1)} all-gather(bf16[128,128]{1,0:T(8,128)(2,1)S(1)} %convolution_convert_fusion), channel_id=1, replica_groups=mesh['dp'=4,'ctx'=16,'tensor'=4] {'ctx'}, dimensions={0}, use_global_device_ids=true | all-gather | bytes 557056 | tf_op jit(solution)/shard_map/all_gather | solution.py:105
  226.7 2.1 while.40
  227.0 1.8 fusion.129
  228.9 0.7 copy-done.7
  229.7 1.1 broadcast.205.clone
  230.8 1.0 broadcast.205
  231.8 7.7 while.41
  232.1 1.5 fusion.140
  233.6 1.3 fusion.141
  235.0 1.3 fusion.142
  236.3 0.8 copy-done.2
  237.6 0.7 constant_dynamic-update-slice_fusion.2
  238.3 1.1 fusion.144
  239.6 0.5 reduce-scatter.7.cloned.1.call-update
  240.1 112.3 %reduce-scatter.5.cloned.1.call-done = f32[128,128]{0,1:T(8,128)} async-done(((f32[2048,128]{0,1:T(8,128)}), f32[128,128]{0,1:T(8,128)}) %reduce-scatter.5.cloned.1.call-update) | async-done | bytes 65552 | tf_op jit(solution)/shard_map/reduce_scatter | solution.py:193
  352.5 1.0 fusion.76
  353.7 84.9 %reduce-scatter.7.cloned.1.call-done = f32[128,128]{1,0:T(8,128)} async-done(((f32[2048,128]{1,0:T(8,128)}), f32[128,128]{1,0:T(8,128)}) %reduce-scatter.7.cloned.1.call-update) | async-done | bytes 65552 | tf_op jit(solution)/shard_map/reduce_scatter | solution.py:194
  438.6 0.8 convert_element_type.76
  439.5 4.5 fusion.57
  444.3 1.3 copy-done.4
  445.6 0.7 fusion.79
  446.4 0.9 copy-done.5
  447.2 2.7 convolution_add_fusion
  450.0 189.2 %reduce-scatter.11.cloned.1.call-done = f32[512,256]{1,0:T(8,128)} async-done(((f32[8192,256]{1,0:T(8,128)}), f32[512,256]{1,0:T(8,128)}) %reduce-scatter.11.cloned.1.call-update) | async-done | bytes 524304 | tf_op jit(solution)/shard_map/reduce_scatter | solution.py:214
  639.4 1.0 copy.67
  640.4 48.8 %reduce-scatter.9.cloned.1.call-done = f32[128,2048]{1,0:T(8,128)} async-done(((f32[128,8192]{1,0:T(8,128)}), f32[128,2048]{1,0:T(8,128)}) %reduce-scatter.9.cloned.1.call-update) | async-done | bytes 1048592 | tf_op jit(solution)/shard_map/reduce_scatter | solution.py:204
  689.2 1.6 fusion.52
  690.8 59.2 %all-reduce.2.cloned.1.call-done = f32[512,256]{1,0:T(8,128)} async-done(((f32[512,256]{1,0:T(8,128)}), f32[512,256]{1,0:T(8,128)}) %all-reduce.2.cloned.1.call-update) | async-done | bytes 524304 | tf_op jit(solution)/shard_map/psum | solution.py:235
  750.0 3.9 multiply_multiply_fusion
  754.1 0.7 add_dynamic-update-slice_fusion
  754.8 75.4 %psum.15 = f32[8192]{0:T(1024)} all-reduce(f32[8192]{0:T(1024)S(1)} %get-tuple-element.461), channel_id=1, replica_groups=mesh['dp'=4,'ctx'=16,'tensor'=4] {'dp','ctx','tensor'}, use_global_device_ids=true, to_apply=%region_19.20 | all-reduce | flops 8192 | bytes 65536 | tf_op jit(solution)/shard_map/psum | solution.py:236
  830.2 3.0 bitcast_reduce_fusion
  833.2 1.1 divide_bitcast_fusion
  (81 shorter events, 3.7 us)
Async XLA Ops:
  7.2 86.4 %all-gather.4.cloned.1.call-start = ((), (), s32[]{:S(2)}) async-start(), calls=%async_computation.4 | async-start | bytes 2228224 | tf_op jit(solution)/shard_map/all_gather | solution.py:88
  11.6 173.5 %all-gather.6.cloned.1.call-start = ((), (), s32[]{:S(2)}) async-start(), calls=%async_computation.5 | async-start | bytes 2228224 | tf_op jit(solution)/shard_map/all_gather | solution.py:89
  12.4 340.1 %reduce-scatter.5.cloned.1.call-start = ((), (), s32[]{:S(2)}) async-start(), calls=%async_computation.6 | async-start | bytes 1114112 | tf_op jit(solution)/shard_map/reduce_scatter | solution.py:193
  13.1 2.1 copy-start.16
  13.1 40.7 %copy-start.12 = (bf16[1,128,1024]{2,1,0:T(8,128)(2,1)S(1)}, bf16[1,128,1024]{2,1,0:T(8,128)(2,1)}, u32[]{:S(2)}) copy-start(bf16[1,128,1024]{2,1,0:T(8,128)(2,1)} %param.17) | copy-start | bytes 786436
  13.1 40.8 %copy-start.13 = (bf16[1,128,1024]{2,1,0:T(8,128)(2,1)S(1)}, bf16[1,128,1024]{2,1,0:T(8,128)(2,1)}, u32[]{:S(2)}) copy-start(bf16[1,128,1024]{2,1,0:T(8,128)(2,1)} %param.23) | copy-start | bytes 786436
  15.2 169.9 %copy-start = (bf16[128,8192]{1,0:T(8,128)(2,1)}, bf16[128,8192]{1,0:T(8,128)(2,1)S(1)}, u32[]{:S(2)}) copy-start(bf16[128,8192]{1,0:T(8,128)(2,1)S(1)} %fusion.51) | copy-start | bytes 6291460
  228.8 0.8 copy-start.7
  236.3 0.8 copy-start.2
  238.3 1.1 copy-start.3
  239.5 200.0 %copy-start.1 = (bf16[128,8192]{1,0:T(8,128)(2,1)S(1)}, bf16[128,8192]{1,0:T(8,128)(2,1)}, u32[]{:S(2)}) copy-start(bf16[128,8192]{1,0:T(8,128)(2,1)} %copy-done) | copy-start | bytes 6291460
  239.5 199.1 %reduce-scatter.7.cloned.1.call-start = ((), (), s32[]{:S(2)}) async-start(), calls=%async_computation.7 | async-start | bytes 1114112 | tf_op jit(solution)/shard_map/reduce_scatter | solution.py:194
  240.1 399.1 %reduce-scatter.11.cloned.1.call-start = ((), (), s32[]{:S(2)}) async-start(), calls=%async_computation.9 | async-start | bytes 8912896 | tf_op jit(solution)/shard_map/reduce_scatter | solution.py:214
  444.0 1.6 copy-start.4
  444.1 245.1 %reduce-scatter.9.cloned.1.call-start = ((), (), s32[]{:S(2)}) async-start(), calls=%async_computation.8 | async-start | bytes 5242880 | tf_op jit(solution)/shard_map/reduce_scatter | solution.py:204
  445.6 1.6 copy-start.5
  449.9 300.1 %all-reduce.2.cloned.1.call-start = ((), (), s32[]{:S(2)}) async-start(), calls=%async_computation.10 | async-start | bytes 1048576 | tf_op jit(solution)/shard_map/psum | solution.py:235
  639.3 110.7 %copy-start.8 = (f32[512,256]{1,0:T(8,128)S(1)}, f32[512,256]{1,0:T(8,128)}, u32[]{:S(2)}) copy-start(f32[512,256]{1,0:T(8,128)} %reduce-scatter.11.cloned.1.call-done) | copy-start | bytes 1572868
  639.3 110.7 %copy-start.10 = (bf16[512,128]{1,0:T(8,128)(2,1)S(1)}, bf16[512,128]{1,0:T(8,128)(2,1)}, u32[]{:S(2)}) copy-start(bf16[512,128]{1,0:T(8,128)(2,1)} %param.19) | copy-start | bytes 393220
  639.3 110.7 %copy-start.11 = (bf16[512,128]{1,0:T(8,128)(2,1)S(1)}, bf16[512,128]{1,0:T(8,128)(2,1)}, u32[]{:S(2)}) copy-start(bf16[512,128]{1,0:T(8,128)(2,1)} %param.18) | copy-start | bytes 393220
  639.3 110.7 %copy-start.14 = (f32[4,128]{1,0:T(4,128)S(1)}, f32[4,128]{1,0:T(4,128)}, u32[]{:S(2)}) copy-start(f32[4,128]{1,0:T(4,128)} %param.21) | copy-start | bytes 6148
  639.4 110.7 %copy-start.15 = (f32[4,128]{1,0:T(4,128)S(1)}, f32[4,128]{1,0:T(4,128)}, u32[]{:S(2)}) copy-start(f32[4,128]{1,0:T(4,128)} %param.20) | copy-start | bytes 6148
  689.2 144.0 %copy-start.6 = (f32[128,2048]{1,0:T(8,128)S(1)}, f32[128,2048]{1,0:T(8,128)}, u32[]{:S(2)}) copy-start(f32[128,2048]{1,0:T(8,128)} %reduce-scatter.9.cloned.1.call-done) | copy-start | bytes 3145732
  750.0 80.2 %copy-start.9 = (f32[512,256]{1,0:T(8,128)S(1)}, f32[512,256]{1,0:T(8,128)}, u32[]{:S(2)}) copy-start(f32[512,256]{1,0:T(8,128)} %all-reduce.2.cloned.1.call-done) | copy-start | bytes 1572868
Sparse Core Ops, SparseCore 0:
  11.7 81.7 all-gather.3
  95.9 89.1 all-gather.5
  239.6 112.8 reduce-scatter.4
  355.0 83.5 reduce-scatter.6
  444.2 194.9 reduce-scatter.10
  641.6 47.5 reduce-scatter.8
  692.0 57.9 all-reduce.1
where the time goes:
time: 842 us; the launch traced here: 841 us
  waiting for transfers between devices  575 us (68%)
  blocking collectives  198 us (24%)
  matrix products  21.6 us (3%)
  other arithmetic  20.2 us (2%)
  between operations  14.4 us (2%)
  local copies, waits for them, and re-layouts  11.7 us (1%)
    reduce_scatter x1, waiting for transfers between devices, body(): lax.psum_scatter(jnp.einsum('td,th->dh', smoothed, both_grads, preferred_...  189 us
    reduce_scatter x1, waiting for transfers between devices, body(): lax.psum_scatter(key_acc, 'ctx', scatter_dimension=0, tiled=True)  112 us
    reduce_scatter x1, waiting for transfers between devices, body(): lax.psum_scatter(value_acc, 'ctx', scatter_dimension=0, tiled=True)  84.9 us
    psum x1, blocking collectives, body(): grad_smoothing = lax.psum(smooth_term, ('dp', 'ctx', 'tensor'))  75.4 us
    psum x1, waiting for transfers between devices, body(): weight_grads = lax.psum(weight_grads, 'dp')  59.2 us
    reduce_scatter x1, waiting for transfers between devices, body(): lax.psum_scatter(d_smoothed, 'tensor', scatter_dimension=1, tiled=True)  48.8 us
    all_gather x1, blocking collectives, body(): lax.all_gather(keys, 'ctx', axis=0, tiled=True)  44.3 us
    all_gather x1, waiting for transfers between devices, body(): lax.all_gather(value_part, 'ctx', axis=0, tiled=True)  39.9 us
  transfers between devices with their start and end apart: 7, of which 7 were waited for; matrix products, arithmetic and copies ran while one was open for 2% of the time, Pallas kernels for 0%

commit v1 on v0

v1 whole, which is shorter than its diff:
```python
import functools
import math

import jax
import jax.numpy as jnp
from jax import lax
from jax.experimental import pallas as pl
from jax.experimental.pallas import tpu as pltpu
from jax.sharding import PartitionSpec as P

HD = 128
GROUP = 128
TWO_PI = 2.0 * math.pi
LOG2E = 1.4426950408889634
MESH = pl.DeviceIdType.MESH
BF = jnp.bfloat16
F32 = jnp.float32
VM = pl.BlockSpec(memory_space=pltpu.VMEM)
ANY = pl.BlockSpec(memory_space=pl.ANY)
DMA = pltpu.SemaphoreType.DMA


def rope_tables(positions):
    half_size = HD // 2
    frequency = jnp.exp(jnp.arange(half_size, dtype=F32) * (-2.0 * math.log(10000.0) / HD))
    angles = positions.astype(F32)[..., None] * frequency
    cosine, sine = jnp.cos(angles), jnp.sin(angles)
    return (
        jnp.concatenate([cosine, cosine], axis=-1),
        jnp.concatenate([-sine, sine], axis=-1),
    )


class Place:
    def __init__(self):
        self.ctx = lax.axis_index("ctx")
        self.dp = lax.axis_index("dp")
        self.y = lax.axis_index("tensor")
        self.x = lax.div(self.ctx, 4)
        self.zl = lax.rem(self.ctx, 4)
        self.zh = lax.div(self.dp, 2)
        self.c = lax.rem(self.dp, 2)
        self.z = self.zh * 4 + self.zl

    def xn(self, d):
        return {"ctx": lax.rem(self.x + (d + 4), 4) * 4 + self.zl, "dp": self.dp}

    def zn(self, d):
        z = lax.rem(self.z + (d + 8), 8)
        return {"ctx": self.x * 4 + lax.rem(z, 4), "dp": lax.div(z, 4) * 2 + self.c}

    def zline(self, d):
        return {"ctx": self.x * 4 + lax.rem(self.zl + d, 4), "dp": self.dp}

    def yn(self, d):
        return {"tensor": lax.rem(self.y + (d + 4), 4)}

    def sib(self):
        return {"dp": self.zh * 2 + (1 - self.c)}

    def far(self, other):
        c = (1 - self.c) if other else self.c
        return {"dp": (1 - self.zh) * 2 + c}

    def mix(self, first, second):
        c = self.c
        return {k: first[k] * (1 - c) + second[k] * c for k in first}


def greet(peers):
    barrier = pltpu.get_barrier_semaphore()
    for peer in peers:
        pl.semaphore_signal(barrier, inc=1, device_id=peer, device_id_type=MESH)
    pl.semaphore_wait(barrier, len(peers))


class Sender:
    def __init__(self, sems):
        self.sems = sems
        self.used = 0
        self.copies = []

    def __call__(self, src, dst, recv, peer):
        copy = pltpu.make_async_remote_copy(
            src_ref=src,
            dst_ref=dst,
            send_sem=self.sems.at[self.used],
            recv_sem=recv,
            device_id=peer,
            device_id_type=MESH,
        )
        self.used += 1
        copy.start()
        self.copies.append(copy)

    def drain(self):
        for copy in self.copies:
            copy.wait_send()
        self.copies = []


def arrived(ref, sem):
    pltpu.make_async_copy(ref, ref, sem).wait()


def proj_kernel(
    part, hid, smooth, cos, sin,
    w_out, smt_out, kv,
    wbuf, sm, smt, acc,
    ssem, nsem, sibsem, zsem, xsem, csem,
):
    p = Place()
    c = p.c
    a0 = p.x * (1 - c) + p.zl * c
    b0 = p.zl * (1 - c) + p.x * c

    def slot(a, b):
        a = lax.rem(a0 + (a + 4), 4)
        b = lax.rem(b0 + (b + 4), 4)
        return (a * 4 + b) * (1 - c) + (b * 4 + a) * c

    an = {d: p.mix(p.xn(d), p.zn(d)) for d in (1, -1)}
    bn = {d: p.mix(p.zn(d), p.xn(d)) for d in (1, -1)}
    sib = p.sib()
    greet([an[1], an[-1], bn[1], bn[-1], sib] + [p.zline(k) for k in (1, 2, 3)])
    send = Sender(ssem)

    def chunk(s, sub):
        return wbuf.at[s * 4 + c * 2 + sub]

    def net(s, sub, peer):
        send(chunk(s, sub), chunk(s, sub), nsem.at[s * 2 + sub], peer)

    def got(s, sub):
        arrived(chunk(s, sub), nsem.at[s * 2 + sub])

    def to_sib(s):
        ref = wbuf.at[pl.ds(s * 4 + c * 2, 2)]
        send(ref, ref, sibsem.at[s], sib)

    def from_sib(s):
        arrived(wbuf.at[pl.ds(s * 4 + (1 - c) * 2, 2)], sibsem.at[s])

    def dot(s, h):
        w = wbuf[pl.ds(s * 4 + h * 2, 2)].reshape(256, 256)
        acc[...] += jnp.dot(sm[s * 2 + h], w, preferred_element_type=F32)

    own = slot(0, 0)
    wbuf[pl.ds(own * 4, 4)] = part[...]
    for sub in (0, 1):
        net(own, sub, an[1])
        net(own, 1 - sub, an[-1])
        net(own, sub, bn[1])
        net(own, 1 - sub, bn[-1])

    inverse = 1.0 / smooth[...]
    for j in range(32):
        cols = slice(j * 256, (j + 1) * 256)
        block = (hid[:, cols].astype(F32) * inverse[:, cols])
        sm[j] = block.astype(BF)
        smt[j] = block.T.astype(BF)
    smt_copy = pltpu.make_async_copy(smt, smt_out, csem.at[0])
    smt_copy.start()
    acc[...] = jnp.zeros_like(acc)
    dot(own, 0)
    dot(own, 1)

    left, right, far = slot(-1, 0), slot(1, 0), slot(2, 0)
    got(left, 0)
    net(left, 0, an[1])
    got(right, 1)
    net(right, 1, an[-1])
    for s, sub in ((left, 0), (right, 1)):
        net(s, sub, bn[1])
        net(s, sub, bn[-1])
    for s, sub in ((left, 1), (right, 0)):
        got(s, sub)
        net(s, sub, bn[1])
        net(s, sub, bn[-1])
        to_sib(s)

    def across(a):
        bl, br = slot(a, -1), slot(a, 1)
        got(bl, 0)
        net(bl, 0, bn[1])
        got(br, 1)
        net(br, 1, bn[-1])
        got(bl, 1)
        got(br, 0)
        to_sib(bl)
        to_sib(br)
        dot(bl, c)
        dot(br, c)

    across(0)
    dot(left, c)
    dot(right, c)
    for sub in (0, 1):
        got(far, sub)
        net(far, sub, bn[1])
        net(far, sub, bn[-1])
    to_sib(far)
    dot(far, c)
    for a in (-1, 1, 2):
        across(a)
    order = [(0, -1), (0, 1)]
    for a in (0, -1, 1, 2):
        s = slot(a, 2)
        got(s, 0)
        got(s, 1)
        to_sib(s)
        dot(s, c)
    for a in (-1, 1, 0, 2):
        for b in (0, -1, 1, 2):
            if a == 0 and b == 0:
                continue
            s = slot(b, a)
            from_sib(s)
            dot(s, 1 - c)

    w_copy = pltpu.make_async_copy(wbuf, w_out, csem.at[1])
    w_copy.start()

    key_raw = acc[:, :HD]
    rotated = key_raw * cos[...] + pltpu.roll(key_raw, HD // 2, 1) * sin[...]
    kv[p.ctx, :, :HD] = rotated.astype(BF)
    kv[p.ctx, :, HD:] = acc[:, HD:].astype(BF)
    for k in (2, 1, 3):
        send(kv.at[p.ctx], kv.at[p.ctx], zsem.at[k - 1], p.zline(k))
    for k in (1, 3, 2):
        arrived(kv.at[p.x * 4 + lax.rem(p.zl + (4 - k), 4)], zsem.at[k - 1])

    def half(d, h):
        return kv.at[pl.ds(lax.rem(p.x + (d + 4), 4) * 4 + h * 2, 2)]

    def xsend(d, h, dirn, which):
        send(half(d, h), half(d, h), xsem.at[which], p.xn(dirn))

    xsend(0, 0, 1, 0)
    xsend(0, 1, -1, 3)
    xsend(0, 1, 1, 1)
    xsend(0, 0, -1, 2)
    arrived(half(-1, 0), xsem.at[0])
    xsend(-1, 0, 1, 4)
    arrived(half(1, 1), xsem.at[3])
    xsend(1, 1, -1, 5)
    arrived(half(-1, 1), xsem.at[1])
    arrived(half(1, 0), xsem.at[2])
    arrived(half(2, 0), xsem.at[4])
    arrived(half(2, 1), xsem.at[5])
    send.drain()
    smt_copy.wait()
    w_copy.wait()


def project(part, hid, smooth, cos, sin):
    return pl.pallas_call(
        proj_kernel,
        name="proj",
        out_shape=(
            jax.ShapeDtypeStruct((64, 128, 256), BF),
            jax.ShapeDtypeStruct((32, 256, 128), BF),
            jax.ShapeDtypeStruct((16, 128, 256), BF),
        ),
        in_specs=[VM] * 5,
        out_specs=(ANY, ANY, VM),
        scratch_shapes=[
            pltpu.VMEM((64, 128, 256), BF),
            pltpu.VMEM((32, 128, 256), BF),
            pltpu.VMEM((32, 256, 128), BF),
            pltpu.VMEM((128, 256), F32),
            DMA((64,)),
            DMA((32,)),
            DMA((16,)),
            DMA((3,)),
            DMA((6,)),
            DMA((2,)),
        ],
        compiler_params=pltpu.CompilerParams(
            collective_id=0, has_side_effects=True, vmem_limit_bytes=40 << 20
        ),
    )(part, hid, smooth, cos, sin)


def attn_kernel(
    kv, queries, dout, start, cos, sin, dkv, gq, qr, qt, do, dot_t, scr, dpr, dq
):
    ctx = lax.axis_index("ctx")
    groups = qr.shape[0] // 128
    scale = HD ** (-0.5)
    for g in range(groups):
        cols = slice(g * 128, (g + 1) * 128)
        q = queries[:, cols].astype(F32)
        q = (q * cos[...] + pltpu.roll(q, HD // 2, 1) * sin[...]).astype(BF)
        qr[cols, :] = q
        qt[:, cols] = q.astype(F32).T.astype(BF)
        d = dout[:, cols]
        do[cols, :] = d
        dot_t[:, cols] = d.astype(F32).T.astype(BF)
    width = 256
    chunks = qr.shape[0] // width
    q_index = ctx * 128 + lax.rem(lax.broadcasted_iota(jnp.int32, (1, width), 1), 128)
    first = start[:, :width]
    row = lax.broadcasted_iota(jnp.int32, (128, width), 0)

    def stats(j, carry):
        kj = kv[j, :, :HD]
        vj = kv[j, :, HD:]
        k_index = row + j * 128
        allowed = (k_index <= q_index) & (k_index >= first)
        out = []
        for n in range(chunks):
            cols = slice(n * width, (n + 1) * width)
            m, l, u = carry[n]
            s = jnp.dot(kj, qt[:, cols], preferred_element_type=F32) * (scale * LOG2E)
            s = jnp.where(allowed, s, -1e30)
            d = jnp.dot(vj, dot_t[:, cols], preferred_element_type=F32)
            scr[j, :, cols] = s
            dpr[j, :, cols] = d
            m_new = jnp.maximum(m, jnp.max(s, axis=0, keepdims=True))
            e = jnp.where(allowed, jnp.exp2(s - m_new), 0.0)
            fix = jnp.exp2(m - m_new)
            l = l * fix + jnp.sum(e, axis=0, keepdims=True)
            u = u * fix + jnp.sum(e * d, axis=0, keepdims=True)
            out.append((m_new, l, u))
        return tuple(out)

    zero = jnp.zeros((1, width), F32)
    carry = lax.fori_loop(
        0, ctx + 1, stats, tuple((zero - 1e30, zero, zero) for _ in range(chunks))
    )
    shift = [m + jnp.log2(l) for m, l, u in carry]
    delta = [u / l for m, l, u in carry]
    dq[...] = jnp.zeros_like(dq)

    def grads(j, _):
        kt = kv[j, :, :HD].astype(F32).T.astype(BF)
        dk = jnp.zeros((128, HD), F32)
        dv = jnp.zeros((128, HD), F32)
        for n in range(chunks):
            cols = slice(n * width, (n + 1) * width)
            prob = jnp.exp2(scr[j, :, cols] - shift[n])
            ds = (prob * (dpr[j, :, cols] - delta[n])).astype(BF)
            dv += jnp.dot(prob.astype(BF), do[cols, :], preferred_element_type=F32)
            dk += jnp.dot(ds, qr[cols, :], preferred_element_type=F32)
            dq[:, cols] += jnp.dot(kt, ds, preferred_element_type=F32)
        dkv[j, :, :HD] = (dk * scale).astype(BF)
        dkv[j, :, HD:] = dv.astype(BF)
        return 0

    lax.fori_loop(0, ctx + 1, grads, 0)

    def clear(j, _):
        dkv[j] = jnp.zeros((128, 2 * HD), BF)
        return 0

    lax.fori_loop(ctx + 1, 16, clear, 0)
    for g in range(groups):
        cols = slice(g * 128, (g + 1) * 128)
        t = dq[:, cols].T * scale
        gq[:, cols] = t * cos[...] - pltpu.roll(t, HD // 2, 1) * sin[...]


def attend(kv, queries, dout, start, cos, sin):
    rows = queries.shape[1]
    return pl.pallas_call(
        attn_kernel,
        name="attn",
        out_shape=(
            jax.ShapeDtypeStruct((16, 128, 256), BF),
            jax.ShapeDtypeStruct((128, rows), F32),
        ),
        in_specs=[VM] * 6,
        out_specs=(VM, VM),
        scratch_shapes=[
            pltpu.VMEM((rows, HD), BF),
            pltpu.VMEM((HD, rows), BF),
            pltpu.VMEM((rows, HD), BF),
            pltpu.VMEM((HD, rows), BF),
            pltpu.VMEM((16, 128, rows), F32),
            pltpu.VMEM((16, 128, rows), F32),
            pltpu.VMEM((HD, rows), F32),
        ],
        compiler_params=pltpu.CompilerParams(vmem_limit_bytes=48 << 20),
    )(kv, queries, dout, start, cos, sin)


def grad_kernel(
    dkv, cos, sin, w_hbm, smt_hbm, ss_hbm, st_hbm, cb_hbm,
    dcol, gkw, gvw, steps, gsm,
    w, smt, ss, st, cb,
    a_r1, a_r2, a_st, a_t, a_zs, a_z,
    hs, hr, ms, r1, r2, sx, tz, zs, zr, fb,
    y_s, y_r1, y_r2, yv, gs,
    ssem, csem, a1sem, a2sem, azsem, hsem, r1sem, r2sem, zsem, fsem,
    y1sem, y2sem, vsem, gxsem, gzsem,
):
    p = Place()
    c = p.c
    loads = [
        pltpu.make_async_copy(s, d, csem.at[i])
        for i, (s, d) in enumerate(
            ((smt_hbm, smt), (w_hbm, w), (ss_hbm, ss), (st_hbm, st), (cb_hbm, cb))
        )
    ]
    for load in loads:
        load.start()
    xr, xl = p.xn(1), p.xn(-1)
    yr, yl = p.yn(1), p.yn(-1)
    sib = p.sib()
    greet(
        [xr, xl, p.xn(2), yr, yl, p.yn(2), sib, p.far(1)] + [p.zn(k) for k in range(1, 8)]
    )
    send = Sender(ssem)

    def xblk(d):
        return lax.rem(p.x + (d + 4), 4)

    def ahalf(d, h):
        return pl.ds(xblk(d) * 4 + h * 2, 2)

    send(dkv.at[ahalf(2, 0)], a_r1.at[0], a1sem.at[0], xr)
    send(dkv.at[ahalf(2, 1)], a_r1.at[1], a1sem.at[1], xl)
    send(dkv.at[ahalf(1, 1)], a_r2.at[0, 1], a2sem.at[1], xr)
    send(dkv.at[ahalf(-1, 0)], a_r2.at[1, 0], a2sem.at[2], xl)
    arrived(a_r1.at[0], a1sem.at[0])
    a_st[0] = (dkv[ahalf(1, 0)].astype(F32) + a_r1[0].astype(F32)).astype(BF)
    send(a_st.at[0], a_r2.at[0, 0], a2sem.at[0], xr)
    arrived(a_r1.at[1], a1sem.at[1])
    a_st[1] = (dkv[ahalf(-1, 1)].astype(F32) + a_r1[1].astype(F32)).astype(BF)
    send(a_st.at[1], a_r2.at[1, 1], a2sem.at[3], xl)
    for i, (s, h) in ((1, (0, 1)), (2, (1, 0)), (0, (0, 0)), (3, (1, 1))):
        arrived(a_r2.at[s, h], a2sem.at[i])
    for h in (0, 1):
        total = (
            dkv[ahalf(0, h)].astype(F32) + a_r2[0, h].astype(F32) + a_r2[1, h].astype(F32)
        )
        a_t[h * 2 : h * 2 + 2] = total
        a_zs[h * 2 : h * 2 + 2] = total.astype(BF)
    for k in (2, 1, 3):
        send(a_zs.at[lax.rem(p.zl + k, 4)], a_z.at[k - 1], azsem.at[k - 1], p.zline(k))
    d_kv = a_t[p.zl]
    for k in (1, 3, 2):
        arrived(a_z.at[k - 1], azsem.at[k - 1])
        d_kv += a_z[k - 1].astype(F32)
    dk = d_kv[:, :HD]
    dk = dk * cos[...] - pltpu.roll(dk, HD // 2, 1) * sin[...]
    g = jnp.concatenate([dk, d_kv[:, HD:]], axis=1).astype(BF)

    dirs = (2, 1, -1, 0)

    def wgrad(k):
        blk = xblk(dirs[k])
        for zl in range(4):
            j = (blk * 4 + zl) * 2
            hs[k, zl] = jnp.dot(smt[j + (1 - c)], g, preferred_element_type=F32).astype(BF)
            ms[k, zl] = jnp.dot(smt[j + c], g, preferred_element_type=F32).astype(BF)
        send(hs.at[k], hr.at[k], hsem.at[k], sib)

    def pair(k, h):
        part = slice(h * 2, h * 2 + 2)
        return ms[k, part].astype(F32) + hr[k, part].astype(F32)

    def dgrad(d, h):
        blk = lax.rem(p.y + (d + 4), 4) * 16 + h * 8
        out = []
        for i in range(4):
            wb = w[pl.ds(blk + i * 2, 2)].reshape(256, 256)
            out.append(
                lax.dot_general(g, wb, (((1,), (1,)), ((), ())), preferred_element_type=F32)
            )
        return out

    def dstore(k, d, h, extra=None):
        for i, piece in enumerate(dgrad(d, h)):
            cols = slice(i * 256, (i + 1) * 256)
            if extra is not None:
                piece = piece + extra[:, cols].astype(F32)
            y_s[k, h, :, cols] = piece.astype(BF)

    loads[0].wait()
    wgrad(0)
    loads[1].wait()
    dstore(0, 2, 0)
    send(y_s.at[0, 0], y_r1.at[0], y1sem.at[0], yr)
    dstore(0, 2, 1)
    send(y_s.at[0, 1], y_r1.at[1], y1sem.at[1], yl)
    wgrad(1)
    arrived(hr.at[0], hsem.at[0])
    for h in (0, 1):
        sx[0, h] = pair(0, h).astype(BF)
        send(sx.at[0, h], r1.at[h], r1sem.at[h], (xr, xl)[h])
    dstore(1, 1, 1)
    send(y_s.at[1, 1], y_r2.at[0, 1], y2sem.at[1], yr)
    dstore(2, -1, 0)
    send(y_s.at[2, 0], y_r2.at[1, 0], y2sem.at[2], yl)
    wgrad(2)
    arrived(hr.at[1], hsem.at[1])
    sx[1, 1] = pair(1, 1).astype(BF)
    send(sx.at[1, 1], r2.at[0, 1], r2sem.at[1], xr)
    arrived(hr.at[2], hsem.at[2])
    sx[2, 0] = pair(2, 0).astype(BF)
    send(sx.at[2, 0], r2.at[1, 0], r2sem.at[2], xl)
    wgrad(3)
    arrived(y_r1.at[0], y1sem.at[0])
    dstore(1, 1, 0, y_r1.at[0])
    send(y_s.at[1, 0], y_r2.at[0, 0], y2sem.at[0], yr)
    arrived(y_r1.at[1], y1sem.at[1])
    dstore(2, -1, 1, y_r1.at[1])
    send(y_s.at[2, 1], y_r2.at[1, 1], y2sem.at[3], yl)
    arrived(r1.at[0], r1sem.at[0])
    sx[1, 0] = (pair(1, 0) + r1[0].astype(F32)).astype(BF)
    send(sx.at[1, 0], r2.at[0, 0], r2sem.at[0], xr)
    arrived(r1.at[1], r1sem.at[1])
    sx[2, 1] = (pair(2, 1) + r1[1].astype(F32)).astype(BF)
    send(sx.at[2, 1], r2.at[1, 1], r2sem.at[3], xl)
    for h in (0, 1):
        for i, piece in enumerate(dgrad(0, h)):
            dcol[:, h * 1024 + i * 256 : h * 1024 + (i + 1) * 256] = piece

    arrived(hr.at[3], hsem.at[3])
    for i, (s, h) in ((1, (0, 1)), (2, (1, 0)), (0, (0, 0)), (3, (1, 1))):
        arrived(r2.at[s, h], r2sem.at[i])
    for h in (0, 1):
        total = pair(3, h) + r2[0, h].astype(F32) + r2[1, h].astype(F32)
        total = total.reshape(4, 128, 256)
        tz[h * 4 : h * 4 + 4] = total
        zs[h * 4 : h * 4 + 4] = total.astype(BF)
    for k in (4, 3, 5, 2, 6, 1, 7):
        z = lax.rem(p.z + k, 8)
        send(zs.at[lax.rem(z, 4) * 2 + lax.div(z, 4)], zr.at[k - 1], zsem.at[k - 1], p.zn(k))

    for i, (s, h) in ((1, (0, 1)), (2, (1, 0)), (0, (0, 0)), (3, (1, 1))):
        arrived(y_r2.at[s, h], y2sem.at[i])
    for h in (0, 1):
        cols = slice(h * 1024, (h + 1) * 1024)
        dcol[:, cols] += y_r2[0, h].astype(F32) + y_r2[1, h].astype(F32)

    f = tz[p.zl * 2 + p.zh]
    for k in (1, 7, 2, 6, 3, 5, 4):
        arrived(zr.at[k - 1], zsem.at[k - 1])
        f += zr[k - 1].astype(F32)
    mine = c * 2 + p.zh
    fb[mine] = f.astype(BF)
    for i, peer in ((0, p.far(0)), (1, p.far(1)), (2, sib)):
        send(fb.at[mine], fb.at[mine], fsem.at[i], peer)
    for load in loads[2:]:
        load.wait()
    arrived(fb.at[(1 - c) * 2 + p.zh], fsem.at[2])
    arrived(fb.at[c * 2 + (1 - p.zh)], fsem.at[0])
    arrived(fb.at[(1 - c) * 2 + (1 - p.zh)], fsem.at[1])
    vec = []
    for q in range(4):
        rows = slice(q * 128, (q + 1) * 128)
        f = fb[q].astype(F32)
        t = f * cb[rows, :]
        t = t[:, :HD] + t[:, HD:]
        vec.append(jnp.sum(t.T, axis=0, keepdims=True))
    yv[p.y] = jnp.concatenate(vec + vec, axis=0)
    for k in (2, 1, 3):
        send(yv.at[p.y], yv.at[p.y], vsem.at[k - 1], p.yn(k))
    for q in range(4):
        rows = slice(q * 128, (q + 1) * 128)
        f = fb[q].astype(F32)
        o = f * ss[rows, :]
        gkw[rows, :] = o[:, :HD]
        gvw[rows, :] = o[:, HD:]
        steps[q : q + 1, :] = jnp.sum(f * st[rows, :], axis=0, keepdims=True)
    for k in (1, 3, 2):
        arrived(yv.at[lax.rem(p.y + (4 - k), 4)], vsem.at[k - 1])
    own = p.zl * 4 + p.x
    gs[own] = (yv[0] + yv[1]) + (yv[2] + yv[3])
    for k in (2, 1, 3):
        send(gs.at[own], gs.at[own], gxsem.at[k - 1], p.xn(k))
    for k in (1, 3, 2):
        arrived(gs.at[p.zl * 4 + lax.rem(p.x + (4 - k), 4)], gxsem.at[k - 1])
    for k in (2, 1, 3):
        row = pl.ds(p.zl * 4, 4)
        send(gs.at[row], gs.at[row], gzsem.at[k - 1], p.zline(k))
    for k in (1, 3, 2):
        arrived(gs.at[pl.ds(lax.rem(p.zl + (4 - k), 4) * 4, 4)], gzsem.at[k - 1])
    for i in range(16):
        gsm[i * 4 : i * 4 + 4, :] = gs[(i % 4) * 4 + i // 4, :4, :]
    send.drain()


def gradients(dkv, cos, sin, w, smt, ss, st, cb):
    return pl.pallas_call(
        grad_kernel,
        name="grads",
        out_shape=(
            jax.ShapeDtypeStruct((128, 2048), F32),
            jax.ShapeDtypeStruct((512, 128), F32),
            jax.ShapeDtypeStruct((512, 128), F32),
            jax.ShapeDtypeStruct((4, 256), F32),
            jax.ShapeDtypeStruct((64, 128), F32),
        ),
        in_specs=[VM] * 3 + [ANY] * 5,
        out_specs=(VM,) * 5,
        scratch_shapes=[
            pltpu.VMEM((64, 128, 256), BF),
            pltpu.VMEM((32, 256, 128), BF),
            pltpu.VMEM((512, 256), F32),
            pltpu.VMEM((512, 256), F32),
            pltpu.VMEM((512, 256), F32),
            pltpu.VMEM((2, 2, 128, 256), BF),
            pltpu.VMEM((2, 2, 2, 128, 256), BF),
            pltpu.VMEM((2, 2, 128, 256), BF),
            pltpu.VMEM((4, 128, 256), F32),
            pltpu.VMEM((4, 128, 256), BF),
            pltpu.VMEM((3, 128, 256), BF),
            pltpu.VMEM((4, 4, 256, 256), BF),
            pltpu.VMEM((4, 4, 256, 256), BF),
            pltpu.VMEM((4, 4, 256, 256), BF),
            pltpu.VMEM((2, 2, 256, 256), BF),
            pltpu.VMEM((2, 2, 2, 256, 256), BF),
            pltpu.VMEM((3, 2, 2, 256, 256), BF),
            pltpu.VMEM((8, 128, 256), F32),
            pltpu.VMEM((8, 128, 256), BF),
            pltpu.VMEM((7, 128, 256), BF),
            pltpu.VMEM((4, 128, 256), BF),
            pltpu.VMEM((3, 2, 128, 1024), BF),
            pltpu.VMEM((2, 128, 1024), BF),
            pltpu.VMEM((2, 2, 128, 1024), BF),
            pltpu.VMEM((4, 8, 128), F32),
            pltpu.VMEM((16, 8, 128), F32),
            DMA((48,)),
            DMA((5,)),
            DMA((2,)),
            DMA((4,)),
            DMA((3,)),
            DMA((4,)),
            DMA((2,)),
            DMA((4,)),
            DMA((7,)),
            DMA((3,)),
            DMA((2,)),
            DMA((4,)),
            DMA((3,)),
            DMA((3,)),
            DMA((3,)),
        ],
        compiler_params=pltpu.CompilerParams(
            collective_id=1, has_side_effects=True, vmem_limit_bytes=56 << 20
        ),
    )(dkv, cos, sin, w, smt, ss, st, cb)


def body(
    hidden_states,
    positions,
    queries,
    key_weight,
    value_weight,
    key_step,
    value_step,
    smoothing,
    grad_out,
):
    shard_index = lax.axis_index("ctx")
    shard_rows = key_weight.shape[0]
    smooth_rows = lax.dynamic_slice_in_dim(smoothing, shard_index * shard_rows, shard_rows)
    weight = jnp.concatenate([key_weight, value_weight], axis=1).astype(F32)
    step = jnp.repeat(jnp.concatenate([key_step, value_step], axis=1), GROUP, axis=0)
    ratio = weight * smooth_rows[:, None] / step
    phase = TWO_PI * ratio
    sine = jnp.sin(phase) / TWO_PI
    cosine = jnp.cos(phase)
    quant = (step * (ratio - sine)).astype(BF)
    slope = 1.0 - cosine
    ss = slope * smooth_rows[:, None]
    st = ratio * cosine - sine
    cb = slope * weight - quant.astype(F32) / smooth_rows[:, None]

    cos, sin = rope_tables(positions[0])
    w, smt, kv = project(
        quant.reshape(4, 128, 256), hidden_states[0], smoothing[None, :], cos, sin
    )
    tok = positions.shape[1]
    start = shard_index * tok + jnp.arange(tok, dtype=jnp.int32) - positions[0]
    start = jnp.tile(start, queries.shape[2] // HD)[None, :]
    dkv, gq = attend(kv, queries[0], grad_out[0], start, cos, sin)
    dcol, gkw, gvw, steps, gsm = gradients(dkv, cos, sin, w, smt, ss, st, cb)
    width = dcol.shape[1]
    smooth_cols = lax.dynamic_slice_in_dim(smoothing, lax.axis_index("tensor") * width, width)
    grad_hidden = (dcol / smooth_cols)[None]
    return (
        grad_hidden,
        gq[None],
        gkw,
        gvw,
        steps[:, :HD],
        steps[:, HD:],
        gsm.reshape(smoothing.shape),
    )


def solution(mesh):
    in_specs = (
        P("dp", "ctx", None),
        P("dp", "ctx"),
        P("dp", "ctx", "tensor"),
        P("ctx", "tensor"),
        P("ctx", "tensor"),
        P("ctx", "tensor"),
        P("ctx", "tensor"),
        P(),
        P("dp", "ctx", "tensor"),
    )
    out_specs = (
        P("dp", "ctx", "tensor"),
        P("dp", "ctx", "tensor"),
        P("ctx", "tensor"),
        P("ctx", "tensor"),
        P("ctx", "tensor"),
        P("ctx", "tensor"),
        P(),
    )
    return jax.shard_map(body, mesh=mesh, in_specs=in_specs, out_specs=out_specs, check_vma=False)
```

time: 842 us -> 160 us (0.19)
  waiting for transfers between devices: 575 us -> 0 us
  blocking collectives: 198 us -> 0 us
  Pallas kernels: 0 us -> 136 us
  matrix products: 21.6 us -> 0 us
  between operations: 14.4 us -> 0.78 us
  other arithmetic: 20.2 us -> 10.5 us
    reduce_scatter x4 -> x0, waiting for transfers between devices: 435 us -> none  [the longest x1 189 us: body(): lax.psum_scatter(jnp.einsum('td,th->dh', smoothed, both_grads, preferred_...]
    pallas_call x0 -> x3, Pallas kernels: none -> 136 us  [the longest x1 89.8 us: gradients(): pl.pallas_call(grad_kernel, name='grads', out_shape=(jax.ShapeDtypeStruct...]
    all_gather x3 -> x0, blocking collectives: 122 us -> none  [the longest x1 44.3 us: body(): lax.all_gather(keys, 'ctx', axis=0, tiled=True)]
    all_gather x2 -> x0, waiting for transfers between devices: 79.2 us -> none  [the longest x1 39.9 us: body(): lax.all_gather(value_part, 'ctx', axis=0, tiled=True)]
    psum x1 -> x0, blocking collectives: 75.4 us -> none  [body(): grad_smoothing = lax.psum(smooth_term, ('dp', 'ctx', 'tensor'))]
    psum x1 -> x0, waiting for transfers between devices: 59.2 us -> none  [body(): weight_grads = lax.psum(weight_grads, 'dp')]
    dot_general x12 -> x0, matrix products: 21.6 us -> none  [the longest x1 4.55 us: body(): jnp.einsum('td,th->dh', smoothed, both_grads, preferred_element_type=jnp....]
  transfers between devices with their start and end apart: 7 -> 0, of which waited for: 7 -> 0; matrix products, arithmetic and copies ran while one was open for 2% -> 0% of each run, Pallas kernels for 0% -> 0%
where the time goes in v1:
time: 160 us; the launch traced here: 159 us
  Pallas kernels  136 us (85%)
  local copies, waits for them, and re-layouts  11.6 us (7%)
  other arithmetic  10.5 us (7%)
    pallas_call x1, Pallas kernels, gradients(): pl.pallas_call(grad_kernel, name='grads', out_shape=(jax.ShapeDtypeStruct...  89.8 us
    pallas_call x1, Pallas kernels, project(): pl.pallas_call(proj_kernel, name='proj', out_shape=(jax.ShapeDtypeStruct(...  44 us
    unnamed x33, local copies, waits for them, and re-layouts  8.66 us
    sub x1, other arithmetic, body(): cb = slope * weight - quant.astype(F32) / smooth_rows[:, None]  3.38 us

profile of v1, /device:TPU:1, one launch (start us, length us, event | category | flops | bytes accessed | tf_op | source)
XLA Modules:
  0.0 159.2 jit_solution(16803270711160911191)
XLA Ops:
  0.6 0.0 copy-start.6
  0.6 0.0 copy-start.7
  0.7 0.7 subtract_bitcast_fusion
  1.4 0.3 fusion.2
  1.7 0.1 pad_maximum_fusion.1
  1.8 0.0 copy-start.3
  1.8 0.0 copy-start.4
  1.9 0.8 dynamic-slice_bitcast_fusion
  2.7 0.7 pad_maximum_fusion.3
  3.4 2.9 %multiply_convert_fusion.part = bf16[4,128,256]{2,1,0:T(8,128)(2,1)S(1)} fusion(bf16[4,128,128]{2,1,0:T(8,128)(2,1)} %bitcast.35, bf16[4,128,128]{2,1,0:T(8,128)(2,1)} %bitcast.36, f32[4,128]{1,0:T(4,128)S(1)} %dynamic-slice_bitcast_fusion, f32[4,256]{1,0:T(4,128)S(1)} %pad_maximum_fusion.3), kind=kLoop, calls=%fused_computation.9 | loop fusion | flops 1441792 | bytes 530432 | tf_op jit(solution)/shard_map/convert_element_type | solution.py:669
  6.3 0.0 copy-start.2
  6.3 1.6 copy-done.2
  7.9 0.0 copy-start.8
  7.9 0.8 copy-done.8
  8.6 0.0 copy-start.9
  8.6 0.0 copy-start.10
  8.6 44.0 %proj.1 = (bf16[64,128,256]{2,1,0:T(8,128)(2,1)S(1)}, bf16[32,256,128]{2,1,0:T(8,128)(2,1)S(1)}, bf16[16,128,256]{2,1,0:T(8,128)(2,1)S(1)}) custom-call(bf16[4,128,256]{2,1,0:T(8,128)(2,1)S(1)} %multiply_convert_fusion.part, bf16[128,8192]{1,0:T(8,128)(2,1)S(1)} %bitcast.30, f32[1,8192]{1,0:T(1,128)S(1)} %bitcast.33, f32[128,128]{1,0:T(8,128)S(1)} %get-tuple-element.37.cos, ...), custom_call_target="tpu_custom_call" | custom-call | tf_op jit(solution)/shard_map/proj/pallas_call | solution.py:257
  52.7 0.0 copy-start
  52.7 1.9 %copy-done = bf16[64,128,256]{2,1,0:T(8,128)(2,1)} copy-done((bf16[64,128,256]{2,1,0:T(8,128)(2,1)}, bf16[64,128,256]{2,1,0:T(8,128)(2,1)S(1)}, u32[]{:S(2)}) %copy-start) | copy-done | bytes 4194328
  54.6 0.0 copy-start.1
  54.6 1.3 copy-done.1
  56.0 0.0 copy-done.6
  56.0 0.0 copy-done.7
  56.0 2.5 %attn.1 = (bf16[16,128,256]{2,1,0:T(8,128)(2,1)S(1)}, f32[128,1024]{1,0:T(8,128)}) custom-call(bf16[16,128,256]{2,1,0:T(8,128)(2,1)S(1)} %get-tuple-element.17.kv, bf16[128,1024]{1,0:T(8,128)(2,1)S(1)} %bitcast.31, bf16[128,1024]{1,0:T(8,128)(2,1)S(1)} %bitcast.32, s32[1,1024]{1,0:T(1,128)S(1)} %bitcast.34, f32[128,128]{1,0:T(8,128)S(1)} %get-tuple-element.37.cos, ...), custom_call_target="tpu_custom_call" | custom-call | tf_op jit(solution)/shard_map/attn/pallas_call | solution.py:366
  58.5 0.0 copy-done.3
  58.5 0.0 copy-done.4
  58.5 0.0 copy-start.5
  58.5 1.0 copy-done.5
  59.5 0.8 dynamic_slice.6
  60.2 0.0 copy-done.9
  60.2 0.0 copy-done.10
  60.2 3.4 %fusion = (f32[512,256]{1,0:T(8,128)}, f32[512,256]{1,0:T(8,128)}, f32[512,256]{1,0:T(8,128)}) fusion(f32[512]{0:T(512)S(1)} %dynamic_slice.6, f32[4,256]{1,0:T(4,128)S(1)} %pad_maximum_fusion.3, bf16[512,128]{1,0:T(8,128)(2,1)S(1)} %copy-done.9, bf16[512,128]{1,0:T(8,128)(2,1)S(1)} %copy-done.10), kind=kLoop, calls=%fused_computation.5 | loop fusion | flops 2490368 | bytes 1841152 | tf_op jit(solution)/shard_map/sub | solution.py:673
  63.6 89.8 %grads.1 = (f32[128,2048]{1,0:T(8,128)}, f32[512,128]{1,0:T(8,128)}, f32[512,128]{1,0:T(8,128)}, f32[4,256]{1,0:T(4,128)}, f32[64,128]{1,0:T(8,128)}) custom-call(bf16[16,128,256]{2,1,0:T(8,128)(2,1)} %copy-done.5, f32[128,128]{1,0:T(8,128)} %copy-done.3, f32[128,128]{1,0:T(8,128)} %copy-done.4, bf16[64,128,256]{2,1,0:T(8,128)(2,1)} %copy-done, ...), custom_call_target="tpu_custom_call" | custom-call | tf_op jit(solution)/shard_map/grads/pallas_call | solution.py:588
  153.5 0.0 copy-start.14
  153.5 0.0 copy-start.12
  153.5 0.0 copy-start.11
  153.5 0.0 copy-start.13
  153.5 0.8 dynamic_slice.7
  154.3 2.3 %divide_bitcast_fusion = f32[1,128,2048]{2,1,0:T(8,128)} fusion(f32[128,2048]{1,0:T(8,128)} %get-tuple-element.21, f32[2048]{0:T(1024)S(1)} %dynamic_slice.7), kind=kLoop, calls=%fused_computation | loop fusion | flops 262144 | bytes 2105344 | tf_op jit(solution)/shard_map/broadcast_in_dim | solution.py:686
  156.6 0.0 copy-done.14
  156.6 0.6 fusion.3
  157.1 0.0 copy-done.12
  157.1 0.7 copy.19
  157.9 0.0 copy-done.11
  157.9 0.7 copy.20
  158.6 0.0 copy-done.13
  158.6 0.6 copy.21
  (2 shorter events, 0.0 us)
Async XLA Ops:
  0.6 55.4 %copy-start.6 = (bf16[1,128,1024]{2,1,0:T(8,128)(2,1)S(1)}, bf16[1,128,1024]{2,1,0:T(8,128)(2,1)}, u32[]{:S(2)}) copy-start(bf16[1,128,1024]{2,1,0:T(8,128)(2,1)} %param.11) | copy-start | bytes 786436
  0.6 55.3 %copy-start.7 = (bf16[1,128,1024]{2,1,0:T(8,128)(2,1)S(1)}, bf16[1,128,1024]{2,1,0:T(8,128)(2,1)}, u32[]{:S(2)}) copy-start(bf16[1,128,1024]{2,1,0:T(8,128)(2,1)} %param.17) | copy-start | bytes 786436
  1.8 56.6 %copy-start.3 = (f32[128,128]{1,0:T(8,128)}, f32[128,128]{1,0:T(8,128)S(1)}, u32[]{:S(2)}) copy-start(f32[128,128]{1,0:T(8,128)S(1)} %get-tuple-element.37.cos) | copy-start | bytes 196612
  1.8 56.6 %copy-start.4 = (f32[128,128]{1,0:T(8,128)}, f32[128,128]{1,0:T(8,128)S(1)}, u32[]{:S(2)}) copy-start(f32[128,128]{1,0:T(8,128)S(1)} %get-tuple-element.38.sin) | copy-start | bytes 196612
  6.3 1.6 %copy-start.2 = (bf16[1,128,8192]{2,1,0:T(8,128)(2,1)S(1)}, bf16[1,128,8192]{2,1,0:T(8,128)(2,1)}, u32[]{:S(2)}) copy-start(bf16[1,128,8192]{2,1,0:T(8,128)(2,1)} %param.9) | copy-start | bytes 6291460
  7.9 0.8 copy-start.8
  8.6 51.6 %copy-start.9 = (bf16[512,128]{1,0:T(8,128)(2,1)S(1)}, bf16[512,128]{1,0:T(8,128)(2,1)}, u32[]{:S(2)}) copy-start(bf16[512,128]{1,0:T(8,128)(2,1)} %param.13) | copy-start | bytes 393220
  8.6 51.6 %copy-start.10 = (bf16[512,128]{1,0:T(8,128)(2,1)S(1)}, bf16[512,128]{1,0:T(8,128)(2,1)}, u32[]{:S(2)}) copy-start(bf16[512,128]{1,0:T(8,128)(2,1)} %param.12) | copy-start | bytes 393220
  52.7 1.9 %copy-start = (bf16[64,128,256]{2,1,0:T(8,128)(2,1)}, bf16[64,128,256]{2,1,0:T(8,128)(2,1)S(1)}, u32[]{:S(2)}) copy-start(bf16[64,128,256]{2,1,0:T(8,128)(2,1)S(1)} %get-tuple-element.19.w_hbm) | copy-start | bytes 12582916
  54.6 1.3 copy-start.1
  58.5 1.0 copy-start.5
  153.5 3.1 %copy-start.14 = (f32[4,256]{1,0:T(4,128)S(1)}, f32[4,256]{1,0:T(4,128)}, u32[]{:S(2)}) copy-start(f32[4,256]{1,0:T(4,128)} %get-tuple-element.25) | copy-start | bytes 12292
  153.5 3.7 %copy-start.12 = (f32[512,128]{1,0:T(8,128)S(1)}, f32[512,128]{1,0:T(8,128)}, u32[]{:S(2)}) copy-start(f32[512,128]{1,0:T(8,128)} %get-tuple-element.48) | copy-start | bytes 786436
  153.5 4.4 %copy-start.11 = (f32[512,128]{1,0:T(8,128)S(1)}, f32[512,128]{1,0:T(8,128)}, u32[]{:S(2)}) copy-start(f32[512,128]{1,0:T(8,128)} %get-tuple-element.49) | copy-start | bytes 786436
  153.5 5.1 %copy-start.13 = (f32[64,128]{1,0:T(8,128)S(1)}, f32[64,128]{1,0:T(8,128)}, u32[]{:S(2)}) copy-start(f32[64,128]{1,0:T(8,128)} %get-tuple-element.26) | copy-start | bytes 98308

commit v2 on v1

v2 whole, which is shorter than its diff:
```python
import functools
import math

import jax
import jax.numpy as jnp
import numpy as np
from jax import lax
from jax.experimental import pallas as pl
from jax.experimental.pallas import tpu as pltpu
from jax.sharding import PartitionSpec as P

HD = 128
GROUP = 128
TWO_PI = 2.0 * math.pi
LOG2E = 1.4426950408889634
SCALE = HD ** (-0.5)
MESH = pl.DeviceIdType.MESH
BF = jnp.bfloat16
F32 = jnp.float32
ANY = pl.BlockSpec(memory_space=pl.ANY)
DMA = pltpu.SemaphoreType.DMA


class Place:
    def __init__(self):
        self.ctx = lax.axis_index("ctx")
        self.dp = lax.axis_index("dp")
        self.y = lax.axis_index("tensor")
        self.x = lax.div(self.ctx, 4)
        self.zl = lax.rem(self.ctx, 4)
        self.zh = lax.div(self.dp, 2)
        self.c = lax.rem(self.dp, 2)
        self.z = self.zh * 4 + self.zl

    def xn(self, d):
        return {"ctx": lax.rem(self.x + (d + 4), 4) * 4 + self.zl, "dp": self.dp}

    def zn(self, d):
        z = lax.rem(self.z + (d + 8), 8)
        return {"ctx": self.x * 4 + lax.rem(z, 4), "dp": lax.div(z, 4) * 2 + self.c}

    def zat(self, z):
        return {"ctx": self.x * 4 + lax.rem(z, 4), "dp": lax.div(z, 4) * 2 + self.c}

    def zline(self, d):
        return {"ctx": self.x * 4 + lax.rem(self.zl + d, 4), "dp": self.dp}

    def yn(self, d):
        return {"tensor": lax.rem(self.y + (d + 4), 4)}

    def sib(self):
        return {"dp": self.zh * 2 + (1 - self.c)}

    def far(self, other):
        c = (1 - self.c) if other else self.c
        return {"dp": (1 - self.zh) * 2 + c}

    def mix(self, first, second, c):
        return {k: first[k] * (1 - c) + second[k] * c for k in first}


class Sender:
    def __init__(self, sems):
        self.sems = sems
        self.used = 0
        self.sent = []

    def make(self, index, what):
        src, dst, recv, peer = what()
        return pltpu.make_async_remote_copy(
            src_ref=src,
            dst_ref=dst,
            send_sem=self.sems.at[index],
            recv_sem=recv,
            device_id=peer,
            device_id_type=MESH,
        )

    def __call__(self, what):
        index = self.used
        self.used += 1
        self.sent.append((index, what))
        self.make(index, what).start()

    def drain(self):
        for index, what in self.sent:
            self.make(index, what).wait_send()


def arrived(ref, sem):
    pltpu.make_async_copy(ref, ref, sem).wait()


def sin_cos_turns(r):
    t = (r - jnp.floor(r + 0.5)) * TWO_PI
    q = t * t
    s = jnp.full_like(t, 1.0)
    for n in (14, 12, 10, 8, 6, 4, 2):
        s = 1.0 - q * s * (1.0 / (n * (n + 1)))
    k = jnp.full_like(t, 1.0)
    for n in (15, 13, 11, 9, 7, 5, 3, 1):
        k = 1.0 - q * k * (1.0 / (n * (n + 1)))
    return s * t, k


def spread(row):
    return jnp.broadcast_to(row, (128, row.shape[1])).T


def main_kernel(
    hid_h, pos_h, q_h, kw_h, vw_h, ks_h, vs_h, smooth_h, do_h, freq_h,
    gh_o, gq_o, gkw_o, gvw_o, gks_o, gvs_o, gsm_o,
    hid, pos, queries, kw, vw, ks, vs, smooth, dout, freq,
    cos, sin, inv, ss, st, cb,
    wbuf, sm, smt, acc, kv,
    qr, qt, do, dot_t, scr, dpr, dq, stm, stl, stu,
    a_st, a_rb, a_t, a_zs, a_z,
    hs, hr, ms, r1, r2, sx, tz, zs, zr, fb,
    y_s, y_r1, y_r2, yv, gs,
    dcol, gq, gkw, gvw, gks, gvs, gsm,
    ssem, csem, osem, nsem, sibsem, kvsem, asem, asend, azsem, hsem, r1sem, r2sem,
    zsem, fsem, y1sem, y2sem, vsem, gxsem, gzsem, gssem,
):
    p = Place()
    c = p.c
    pairs = (
        (kw_h, kw), (vw_h, vw), (ks_h, ks), (vs_h, vs), (smooth_h, smooth),
        (pos_h, pos), (freq_h, freq), (hid_h, hid), (q_h, queries), (do_h, dout),
    )
    loads = [pltpu.make_async_copy(s, d, csem.at[i]) for i, (s, d) in enumerate(pairs)]
    for load in loads:
        load.start()
    xr, xl, yr, yl, sib = p.xn(1), p.xn(-1), p.yn(1), p.yn(-1), p.sib()
    peers = [xr, xl, p.xn(2), yr, yl, p.yn(2), sib, p.far(1)]
    peers += [p.zn(k) for k in range(1, 8)]
    barrier = pltpu.get_barrier_semaphore()
    for peer in peers:
        pl.semaphore_signal(barrier, inc=1, device_id=peer, device_id_type=MESH)
    send = Sender(ssem)

    a0 = p.x * (1 - c) + p.zl * c
    b0 = p.zl * (1 - c) + p.x * c

    def slot(a, b):
        a = lax.rem(a0 + (a + 4), 4)
        b = lax.rem(b0 + (b + 4), 4)
        return (a * 4 + b) * (1 - c) + (b * 4 + a) * c

    own = slot(0, 0)
    for load in loads[:5]:
        load.wait()
    for q in range(4):
        rows = slice(q * 128, (q + 1) * 128)
        s_row = smooth[:, pl.ds(pl.multiple_of(p.ctx * 512 + q * 128, 128), 128)]
        s_col = spread(s_row)
        for half, (w_ref, step_ref) in enumerate(((kw, ks), (vw, vs))):
            cols = slice(half * HD, (half + 1) * HD)
            weight = w_ref[rows, :].astype(F32)
            step = step_ref[q : q + 1, :]
            ratio = weight * s_col / step
            sine, cosine = sin_cos_turns(ratio)
            sine = sine * (1.0 / TWO_PI)
            quant = (step * (ratio - sine)).astype(BF)
            wbuf[own * 4 + q, :, cols] = quant
            slope = 1.0 - cosine
            ss[rows, cols] = slope * s_col
            st[rows, cols] = ratio * cosine - sine
            cb[rows, cols] = slope * weight - quant.astype(F32) / s_col
    pl.semaphore_wait(barrier, len(peers))

    an = {d: p.mix(p.xn(d), p.zn(d), c) for d in (1, -1)}
    bn = {d: p.mix(p.zn(d), p.xn(d), c) for d in (1, -1)}

    def chunk(s, sub):
        return wbuf.at[s * 4 + c * 2 + sub]

    def net(s, sub, peer):
        send(lambda: (chunk(s, sub), chunk(s, sub), nsem.at[s * 2 + sub], peer))

    def got(s, sub):
        arrived(chunk(s, sub), nsem.at[s * 2 + sub])

    def to_sib(s):
        ref = wbuf.at[pl.ds(s * 4 + c * 2, 2)]
        send(lambda: (ref, ref, sibsem.at[s], sib))

    def from_sib(s):
        arrived(wbuf.at[pl.ds(s * 4 + (1 - c) * 2, 2)], sibsem.at[s])

    def dot(s, h):
        w = wbuf[pl.ds(s * 4 + h * 2, 2)].reshape(256, 256)
        acc[...] += jnp.dot(sm[s * 2 + h], w, preferred_element_type=F32)

    for sub in (0, 1):
        net(own, sub, an[1])
        net(own, 1 - sub, an[-1])
        net(own, sub, bn[1])
        net(own, 1 - sub, bn[-1])

    def prepare(j0, j1):
        for j in range(j0, j1):
            cols = slice(j * 256, (j + 1) * 256)
            block = hid[:, cols].astype(F32) * inv[:, cols]
            sm[j] = block.astype(BF)
            smt[j] = block.T.astype(BF)

    inv[...] = 1.0 / smooth[...]
    for load in loads[5:7]:
        load.wait()
    angle = spread(pos[...].astype(F32)) * freq[...]
    cos[...] = jnp.cos(angle)
    turned = jnp.sin(angle)
    lane = lax.broadcasted_iota(jnp.int32, (128, 128), 1)
    sin[...] = jnp.where(lane < HD // 2, -turned, turned)

    left, right, far = slot(-1, 0), slot(1, 0), slot(2, 0)
    got(left, 0)
    net(left, 0, an[1])
    got(right, 1)
    net(right, 1, an[-1])
    for s, sub in ((left, 0), (right, 1)):
        net(s, sub, bn[1])
        net(s, sub, bn[-1])
    loads[7].wait()
    prepare(0, 8)
    for s, sub in ((left, 1), (right, 0)):
        got(s, sub)
        net(s, sub, bn[1])
        net(s, sub, bn[-1])
        to_sib(s)

    def across(a):
        bl, br = slot(a, -1), slot(a, 1)
        got(bl, 0)
        net(bl, 0, bn[1])
        got(br, 1)
        net(br, 1, bn[-1])
        got(bl, 1)
        got(br, 0)
        to_sib(bl)
        to_sib(br)
        return bl, br

    ready = [*across(0), left, right]
    for sub in (0, 1):
        got(far, sub)
        net(far, sub, bn[1])
        net(far, sub, bn[-1])
    to_sib(far)
    ready.append(far)
    prepare(8, 20)
    ready += across(-1)
    prepare(20, 32)
    acc[...] = jnp.zeros_like(acc)
    dot(own, 0)
    dot(own, 1)
    ready += across(1)
    for s in ready[:5]:
        dot(s, c)
    ready += across(2)
    for s in ready[5:]:
        dot(s, c)
    for a in (0, -1, 1, 2):
        s = slot(a, 2)
        got(s, 0)
        got(s, 1)
        to_sib(s)
        dot(s, c)
    for a in (-1, 1, 0, 2):
        for b in (0, -1, 1, 2):
            if a == 0 and b == 0:
                continue
            s = slot(b, a)
            from_sib(s)
            dot(s, 1 - c)

    key_raw = acc[:, :HD]
    rotated = key_raw * cos[...] + pltpu.roll(key_raw, HD // 2, 1) * sin[...]
    kv[p.ctx, :, :HD] = rotated.astype(BF)
    kv[p.ctx, :, HD:] = acc[:, HD:].astype(BF)

    def kslot(d, k):
        return lax.rem(p.x + (d + 4), 4) * 4 + lax.rem(p.zl + k, 4)

    def ksend(d, k, peer):
        def what():
            s = kslot(d, k)
            return kv.at[s], kv.at[s], kvsem.at[s], peer()

        send(what)

    def kgot(d, k):
        s = kslot(d, k)
        arrived(kv.at[s], kvsem.at[s])

    to_right, to_left = (lambda: p.xn(1)), (lambda: p.xn(-1))
    ksend(0, 0, to_right)
    ksend(0, 0, to_left)
    for k in (2, 1, 3):
        ksend(0, 0, functools.partial(p.zline, k))

    groups = qr.shape[0] // 128
    for load in loads[8:]:
        load.wait()
    for g in range(groups):
        cols = slice(g * 128, (g + 1) * 128)
        q = queries[:, cols].astype(F32)
        q = q * cos[...] + pltpu.roll(q, HD // 2, 1) * sin[...]
        qr[cols, :] = q.astype(BF)
        qt[:, cols] = q.T.astype(BF)
        d = dout[:, cols]
        do[cols, :] = d
        dot_t[:, cols] = d.astype(F32).T.astype(BF)
    width = 256
    chunks = qr.shape[0] // width
    q_index = p.ctx * 128 + lax.rem(lax.broadcasted_iota(jnp.int32, (1, width), 1), 128)
    first = q_index - jnp.concatenate([pos[...]] * (width // 128), axis=1)
    row = lax.broadcasted_iota(jnp.int32, (256, width), 0)
    stm[...] = jnp.full_like(stm, -1e30)
    stl[...] = jnp.zeros_like(stl)
    stu[...] = jnp.zeros_like(stu)

    def stats(j):
        kj = kv[pl.ds(j * 2, 2), :, :HD].reshape(256, HD)
        vj = kv[pl.ds(j * 2, 2), :, HD:].reshape(256, HD)
        k_index = row + j * 256
        allowed = (k_index <= q_index) & (k_index >= first)
        for n in range(chunks):
            cols = slice(n * width, (n + 1) * width)
            m = stm[:, cols]
            s = jnp.dot(kj, qt[:, cols], preferred_element_type=F32) * (SCALE * LOG2E)
            s = jnp.where(allowed, s, -1e30)
            d = jnp.dot(vj, dot_t[:, cols], preferred_element_type=F32)
            scr[j, :, cols] = s
            dpr[j, :, cols] = d
            m_new = jnp.maximum(m, jnp.max(s, axis=0, keepdims=True))
            e = jnp.where(allowed, jnp.exp2(s - m_new), 0.0)
            fix = jnp.exp2(m - m_new)
            stm[:, cols] = m_new
            stl[:, cols] = stl[:, cols] * fix + jnp.sum(e, axis=0, keepdims=True)
            stu[:, cols] = stu[:, cols] * fix + jnp.sum(e * d, axis=0, keepdims=True)

    def group_step(g, _):
        @pl.when(g == 0)
        def _():
            for k in (1, 3, 2):
                kgot(0, k)
                ksend(0, k, to_right)
                ksend(0, k, to_left)

        @pl.when(g == 1)
        def _():
            for k in (0, 1, 3, 2):
                kgot(-1, k)
                if k in (0, 2):
                    ksend(-1, k, to_right)
                kgot(1, k)
                if k in (1, 3):
                    ksend(1, k, to_left)

        @pl.when(g == 3)
        def _():
            for k in (0, 1, 3, 2):
                kgot(2, k)

        d = g + lax.div(g, 2) - 2 * lax.div(g, 3)

        def pair_step(r, _):
            j = lax.rem(p.x + d, 4) * 2 + r

            @pl.when(j * 2 <= p.ctx)
            def _():
                stats(j)

            return 0

        return lax.fori_loop(0, 2, pair_step, 0)

    lax.fori_loop(0, 4, group_step, 0)

    shift = [stm[:, n * width : (n + 1) * width] for n in range(chunks)]
    delta = []
    for n in range(chunks):
        cols = slice(n * width, (n + 1) * width)
        shift[n] = shift[n] + jnp.log2(stl[:, cols])
        delta.append(stu[:, cols] / stl[:, cols])
    for n in range(chunks):
        cols = slice(n * width, (n + 1) * width)
        stm[:, cols] = shift[n]
        stu[:, cols] = delta[n]
    dq[...] = jnp.zeros_like(dq)

    def acopy(t):
        peer = p.mix(p.xn(1), p.xn(-1), lax.rem(t, 2))
        return pltpu.make_async_remote_copy(
            src_ref=a_st.at[t],
            dst_ref=a_rb.at[t],
            send_sem=asend.at[t],
            recv_sem=asem.at[t],
            device_id=peer,
            device_id_type=MESH,
        )

    def grads(t, _):
        q, r = lax.div(t, 2), lax.rem(t, 2)
        middle = lax.div(q * (3 - q), 2)
        d = middle * (1 + 2 * r) + (1 - middle) * lax.div((3 - q) * 2, 3)
        flip = middle * (2 - q)
        h = r + flip * (1 - 2 * r)
        j = lax.rem(p.x + d, 4) * 2 + h

        @pl.when(j * 2 <= p.ctx)
        def _():
            kj = kv[pl.ds(j * 2, 2), :, :HD].reshape(256, HD)
            kt = kj.astype(F32).T.astype(BF)
            dk = jnp.zeros((256, HD), F32)
            dv = jnp.zeros((256, HD), F32)
            for n in range(chunks):
                cols = slice(n * width, (n + 1) * width)
                prob = jnp.exp2(scr[j, :, cols] - stm[:, cols])
                ds = (prob * (dpr[j, :, cols] - stu[:, cols])).astype(BF)
                dv += jnp.dot(prob.astype(BF), do[cols, :], preferred_element_type=F32)
                dk += jnp.dot(ds, qr[cols, :], preferred_element_type=F32)
                dq[:, cols] += jnp.dot(kt, ds, preferred_element_type=F32)
            a_st[t, :, :, :HD] = (dk * SCALE).astype(BF).reshape(2, 128, HD)
            a_st[t, :, :, HD:] = dv.astype(BF).reshape(2, 128, HD)

        @pl.when(j * 2 > p.ctx)
        def _():
            a_st[t] = jnp.zeros((2, 128, 2 * HD), BF)

        @pl.when(q == 2)
        def _():
            arrived(a_rb.at[t - 4], asem.at[t - 4])
            a_st[t] = (a_st[t].astype(F32) + a_rb[t - 4].astype(F32)).astype(BF)

        @pl.when(t < 6)
        def _():
            acopy(t).start()

        return 0

    lax.fori_loop(0, 8, grads, 0)

    for g in range(groups):
        cols = slice(g * 128, (g + 1) * 128)
        t = dq[:, cols].T * SCALE
        gq[:, cols] = t * cos[...] - pltpu.roll(t, HD // 2, 1) * sin[...]
    stores = [pltpu.make_async_copy(gq, gq_o, osem.at[0])]
    stores[0].start()

    for t in (2, 3, 4, 5):
        arrived(a_rb.at[t], asem.at[t])
    for h, (near, run) in enumerate(((3, 4), (2, 5))):
        total = a_st[6 + h].astype(F32) + a_rb[near].astype(F32) + a_rb[run].astype(F32)
        a_t[h * 2 : h * 2 + 2] = total
        a_zs[h * 2 : h * 2 + 2] = total.astype(BF)
    for k in (2, 1, 3):
        send(
            functools.partial(
                lambda k: (
                    a_zs.at[lax.rem(p.zl + k, 4)], a_z.at[k - 1], azsem.at[k - 1], p.zline(k)
                ),
                k,
            )
        )
    d_kv = a_t[p.zl]
    for k in (1, 3, 2):
        arrived(a_z.at[k - 1], azsem.at[k - 1])
        d_kv += a_z[k - 1].astype(F32)
    dk = d_kv[:, :HD]
    dk = dk * cos[...] - pltpu.roll(dk, HD // 2, 1) * sin[...]
    g = jnp.concatenate([dk, d_kv[:, HD:]], axis=1).astype(BF)

    dirs = (2, 1, -1, 0)

    def wgrad(k):
        blk = lax.rem(p.x + (dirs[k] + 4), 4)
        for zl in range(4):
            j = (blk * 4 + zl) * 2
            his = jnp.dot(smt[j + (1 - c)], g, preferred_element_type=F32).astype(BF)
            mine = jnp.dot(smt[j + c], g, preferred_element_type=F32).astype(BF)
            for u in (0, 1):
                hs[u, k, zl] = his[u * 128 : u * 128 + 128]
                ms[u, k, zl] = mine[u * 128 : u * 128 + 128]

    def hsend(u, k):
        send(lambda: (hs.at[u, k], hr.at[u, k], hsem.at[u, k], sib))

    def hgot(u, k):
        arrived(hr.at[u, k], hsem.at[u, k])

    def both(u, k, h):
        part = slice(h * 2, h * 2 + 2)
        return ms[u, k, part].astype(F32) + hr[u, k, part].astype(F32)

    def xstage(u, k, h, extra=None):
        value = both(u, k, h)
        if extra is not None:
            value = value + extra.astype(F32)
        sx[u, k, h] = value.astype(BF)

    def xfirst(u):
        hgot(u, 0)
        for h in (0, 1):
            xstage(u, 0, h)
            peer = (xr, xl)[h]
            send(
                functools.partial(
                    lambda h, peer: (sx.at[u, 0, h], r1.at[u, h], r1sem.at[u, h], peer), h, peer
                )
            )

    def xraw(u):
        hgot(u, 1)
        xstage(u, 1, 1)
        send(lambda: (sx.at[u, 1, 1], r2.at[u, 0, 1], r2sem.at[u, 1], xr))
        hgot(u, 2)
        xstage(u, 2, 0)
        send(lambda: (sx.at[u, 2, 0], r2.at[u, 1, 0], r2sem.at[u, 2], xl))

    def xrun(u):
        arrived(r1.at[u, 0], r1sem.at[u, 0])
        xstage(u, 1, 0, r1[u, 0])
        send(lambda: (sx.at[u, 1, 0], r2.at[u, 0, 0], r2sem.at[u, 0], xr))
        arrived(r1.at[u, 1], r1sem.at[u, 1])
        xstage(u, 2, 1, r1[u, 1])
        send(lambda: (sx.at[u, 2, 1], r2.at[u, 1, 1], r2sem.at[u, 3], xl))

    def zsend(u):
        hgot(u, 3)
        for i, (s, h) in ((1, (0, 1)), (2, (1, 0)), (0, (0, 0)), (3, (1, 1))):
            arrived(r2.at[u, s, h], r2sem.at[u, i])
        for h in (0, 1):
            total = both(u, 3, h) + r2[u, 0, h].astype(F32) + r2[u, 1, h].astype(F32)
            tz[u, h * 2 : h * 2 + 2] = total
            zs[u, h * 2 : h * 2 + 2] = total.astype(BF)

        def what(k):
            zl = lax.rem(p.zl + k, 4)
            return zs.at[u, zl], zr.at[p.z], zsem.at[p.z], p.zat(u * 4 + zl)

        for k in (2, 1, 3):
            send(functools.partial(what, k))

        @pl.when(p.zh != u)
        def _():
            Sender.make(send, 60 + u, lambda: what(0)).start()

    def dgrad(d, h):
        blk = lax.rem(p.y + (d + 4), 4) * 16 + h * 8
        out = []
        for i in range(4):
            wb = wbuf[pl.ds(blk + i * 2, 2)].reshape(256, 256)
            out.append(
                lax.dot_general(g, wb, (((1,), (1,)), ((), ())), preferred_element_type=F32)
            )
        return out

    def dstore(k, d, h, extra=None):
        for i, piece in enumerate(dgrad(d, h)):
            cols = slice(i * 256, (i + 1) * 256)
            if extra is not None:
                piece = piece + extra[:, cols].astype(F32)
            y_s[k, h, :, cols] = piece.astype(BF)

    for k in range(4):
        wgrad(k)
        hsend(0, k)
    for k in range(4):
        hsend(1, k)
    xfirst(0)
    xraw(0)
    dstore(0, 2, 0)
    send(lambda: (y_s.at[0, 0], y_r1.at[0], y1sem.at[0], yr))
    xrun(0)
    xfirst(1)
    xraw(1)
    dstore(0, 2, 1)
    send(lambda: (y_s.at[0, 1], y_r1.at[1], y1sem.at[1], yl))
    dstore(1, 1, 1)
    send(lambda: (y_s.at[1, 1], y_r2.at[0, 1], y2sem.at[1], yr))
    dstore(2, -1, 0)
    send(lambda: (y_s.at[2, 0], y_r2.at[1, 0], y2sem.at[2], yl))
    xrun(1)
    arrived(y_r1.at[0], y1sem.at[0])
    dstore(1, 1, 0, y_r1.at[0])
    send(lambda: (y_s.at[1, 0], y_r2.at[0, 0], y2sem.at[0], yr))
    zsend(0)
    arrived(y_r1.at[1], y1sem.at[1])
    dstore(2, -1, 1, y_r1.at[1])
    send(lambda: (y_s.at[2, 1], y_r2.at[1, 1], y2sem.at[3], yl))
    for h in (0, 1):
        for i, piece in enumerate(dgrad(0, h)):
            dcol[:, h * 1024 + i * 256 : h * 1024 + (i + 1) * 256] = piece
    zsend(1)

    mine = c * 2 + p.zh
    f = tz[p.zh, p.zl]
    for k in (1, 7, 2, 6, 3, 5, 4):
        z = lax.rem(p.z + k, 8)
        arrived(zr.at[z], zsem.at[z])
        f += zr[z].astype(F32)
    fb[mine] = f.astype(BF)
    for i, peer in ((0, p.far(0)), (1, p.far(1)), (2, sib)):
        send(
            functools.partial(lambda i, peer: (fb.at[mine], fb.at[mine], fsem.at[i], peer), i, peer)
        )

    t = f * cb[pl.ds(pl.multiple_of(mine * 128, 128), 128), :]
    t = t[:, :HD] + t[:, HD:]
    yv[p.y] = jnp.broadcast_to(jnp.sum(t.T, axis=0, keepdims=True), (8, 128))
    for k in (2, 1, 3):
        send(functools.partial(lambda k: (yv.at[p.y], yv.at[p.y], vsem.at[k - 1], p.yn(k)), k))

    for i, (s, h) in ((1, (0, 1)), (2, (1, 0)), (0, (0, 0)), (3, (1, 1))):
        arrived(y_r2.at[s, h], y2sem.at[i])
    inv_cols = inv[:, pl.ds(pl.multiple_of(p.y * 2048, 2048), 2048)]
    for h in (0, 1):
        cols = slice(h * 1024, (h + 1) * 1024)
        total = dcol[:, cols] + y_r2[0, h].astype(F32) + y_r2[1, h].astype(F32)
        dcol[:, cols] = total * inv_cols[:, cols]
    stores.append(pltpu.make_async_copy(dcol, gh_o, osem.at[1]))
    stores[-1].start()

    for k in (1, 3, 2):
        arrived(yv.at[lax.rem(p.y + (4 - k), 4)], vsem.at[k - 1])
    gs[c, p.z, p.x] = (yv[0] + yv[1]) + (yv[2] + yv[3])
    for k in (2, 1, 3):
        send(
            functools.partial(
                lambda k: (
                    gs.at[c, p.z, p.x], gs.at[c, p.z, p.x], gxsem.at[k - 1], p.xn(k)
                ),
                k,
            )
        )
    for k in (1, 3, 2):
        arrived(gs.at[c, p.z, lax.rem(p.x + (4 - k), 4)], gxsem.at[k - 1])
    for k in (4, 3, 5, 2, 6, 1, 7):
        send(
            functools.partial(
                lambda k: (gs.at[c, p.z], gs.at[c, p.z], gzsem.at[k - 1], p.zn(k)), k
            )
        )

    arrived(fb.at[(1 - c) * 2 + p.zh], fsem.at[2])
    arrived(fb.at[c * 2 + (1 - p.zh)], fsem.at[0])
    arrived(fb.at[(1 - c) * 2 + (1 - p.zh)], fsem.at[1])
    for q in range(4):
        rows = slice(q * 128, (q + 1) * 128)
        f = fb[q].astype(F32)
        o = f * ss[rows, :]
        gkw[rows, :] = o[:, :HD]
        gvw[rows, :] = o[:, HD:]
        o = jnp.sum(f * st[rows, :], axis=0, keepdims=True)
        gks[q : q + 1, :] = o[:, :HD]
        gvs[q : q + 1, :] = o[:, HD:]
    for i, (src, dst) in enumerate(((gkw, gkw_o), (gvw, gvw_o), (gks, gks_o), (gvs, gvs_o))):
        stores.append(pltpu.make_async_copy(src, dst, osem.at[2 + i]))
        stores[-1].start()

    for k in (1, 7, 2, 6, 3, 5, 4):
        arrived(gs.at[c, lax.rem(p.z + (8 - k), 8)], gzsem.at[k - 1])
    send(lambda: (gs.at[c], gs.at[c], gssem.at[0], sib))
    arrived(gs.at[1 - c], gssem.at[0])
    for i in range(16):
        for q in range(4):
            r = i * 4 + q
            gsm[r : r + 1, :] = gs[q // 2, (q % 2) * 4 + i % 4, i // 4, :1, :]
    stores.append(pltpu.make_async_copy(gsm, gsm_o, osem.at[6]))
    stores[-1].start()

    send.drain()
    for u in (0, 1):

        @pl.when(p.zh != u)
        def _():
            send.make(
                60 + u, lambda: (zs.at[u, p.zl], zr.at[p.z], zsem.at[p.z], p.zat(u * 4 + p.zl))
            ).wait_send()

    for t in range(6):
        acopy(t).wait_send()
    for store in stores:
        store.wait()


def main_call(*args):
    rows = args[2].shape[1]
    outs = (
        ((128, 2048), F32), ((128, rows), F32), ((512, 128), F32), ((512, 128), F32),
        ((4, 128), F32), ((4, 128), F32), ((64, 128), F32),
    )
    scratch = [pltpu.VMEM(a.shape, a.dtype) for a in args]
    scratch += [pltpu.VMEM(*s) for s in (
        ((128, 128), F32), ((128, 128), F32), ((1, 8192), F32),
        ((512, 256), F32), ((512, 256), F32), ((512, 256), F32),
        ((64, 128, 256), BF), ((32, 128, 256), BF), ((32, 256, 128), BF), ((128, 256), F32),
        ((16, 128, 256), BF),
        ((rows, HD), BF), ((HD, rows), BF), ((rows, HD), BF), ((HD, rows), BF),
        ((8, 256, rows), F32), ((8, 256, rows), F32), ((HD, rows), F32),
        ((1, rows), F32), ((1, rows), F32), ((1, rows), F32),
        ((8, 2, 128, 256), BF), ((6, 2, 128, 256), BF), ((4, 128, 256), F32),
        ((4, 128, 256), BF), ((3, 128, 256), BF),
        ((2, 4, 4, 128, 256), BF), ((2, 4, 4, 128, 256), BF), ((2, 4, 4, 128, 256), BF),
        ((2, 2, 2, 128, 256), BF), ((2, 2, 2, 2, 128, 256), BF), ((2, 3, 2, 2, 128, 256), BF),
        ((2, 4, 128, 256), F32), ((2, 4, 128, 256), BF), ((8, 128, 256), BF),
        ((4, 128, 256), BF),
        ((3, 2, 128, 1024), BF), ((2, 128, 1024), BF), ((2, 2, 128, 1024), BF),
        ((4, 8, 128), F32), ((2, 8, 4, 8, 128), F32),
    )]
    scratch += [pltpu.VMEM(*o) for o in outs]
    scratch += [DMA(s) for s in (
        (128,), (10,), (7,), (32,), (16,), (16,), (6,), (6,), (3,), (2, 4), (2, 2), (2, 4),
        (8,), (3,), (2,), (4,), (3,), (3,), (7,), (1,),
    )]
    return pl.pallas_call(
        main_kernel,
        name="main",
        out_shape=tuple(jax.ShapeDtypeStruct(*o) for o in outs),
        in_specs=[ANY] * len(args),
        out_specs=(ANY,) * len(outs),
        scratch_shapes=scratch,
        compiler_params=pltpu.CompilerParams(
            collective_id=0, has_side_effects=True, vmem_limit_bytes=60 << 20
        ),
    )(*args)


def finish_kernel(*refs):
    count = (len(refs) - 1) // 3
    sems = refs[-1]
    loads, stores = [], []
    for i in range(count):
        held = refs[2 * count + i]
        loads.append(pltpu.make_async_copy(refs[i], held, sems.at[0, i]))
        stores.append(pltpu.make_async_copy(held, refs[count + i], sems.at[1, i]))
    for load in loads:
        load.start()
    for load, store in zip(loads, stores):
        load.wait()
        store.start()
    for store in stores:
        store.wait()


def finish(*arrays):
    return pl.pallas_call(
        finish_kernel,
        name="finish",
        out_shape=tuple(jax.ShapeDtypeStruct(a.shape, a.dtype) for a in arrays),
        in_specs=[ANY] * len(arrays),
        out_specs=(ANY,) * len(arrays),
        scratch_shapes=[pltpu.VMEM(a.shape, a.dtype) for a in arrays] + [DMA((2, len(arrays)))],
        compiler_params=pltpu.CompilerParams(vmem_limit_bytes=60 << 20),
    )(*arrays)


def body(
    hidden_states,
    positions,
    queries,
    key_weight,
    value_weight,
    key_step,
    value_step,
    smoothing,
    grad_out,
):
    index = np.arange(HD) % (HD // 2)
    freq = jnp.asarray((10000.0 ** (-2.0 * index / HD)).astype(np.float32))[None, :]
    gh, gq, gkw, gvw, gks, gvs, gsm = finish(
        *main_call(
            hidden_states[0], positions, queries[0], key_weight, value_weight, key_step,
            value_step, smoothing[None, :], grad_out[0], freq,
        )
    )
    return gh[None], gq[None], gkw, gvw, gks, gvs, gsm.reshape(smoothing.shape)


def solution(mesh):
    in_specs = (
        P("dp", "ctx", None),
        P("dp", "ctx"),
        P("dp", "ctx", "tensor"),
        P("ctx", "tensor"),
        P("ctx", "tensor"),
        P("ctx", "tensor"),
        P("ctx", "tensor"),
        P(),
        P("dp", "ctx", "tensor"),
    )
    out_specs = (
        P("dp", "ctx", "tensor"),
        P("dp", "ctx", "tensor"),
        P("ctx", "tensor"),
        P("ctx", "tensor"),
        P("ctx", "tensor"),
        P("ctx", "tensor"),
        P(),
    )
    return jax.shard_map(body, mesh=mesh, in_specs=in_specs, out_specs=out_specs, check_vma=False)
```

time: 160 us -> 124 us (0.78)
  Pallas kernels: 136 us -> 123 us
  local copies, waits for them, and re-layouts: 11.6 us -> 0 us
  other arithmetic: 10.5 us -> 0 us
    pallas_call x3 -> x2, Pallas kernels: 136 us -> 123 us  [the longest x1 121 us: main_call(): pl.pallas_call(main_kernel, name='main', out_shape=tuple((jax.ShapeDtypeS...]
    unnamed x33 -> x0, local copies, waits for them, and re-layouts: 8.66 us -> none
    sub x1 -> x0, other arithmetic: 3.38 us -> none  [body(): cb = slope * weight - quant.astype(F32) / smooth_rows[:, None]]
    convert_element_type x1 -> x0, other arithmetic: 2.92 us -> none  [body(): quant = (step * (ratio - sine)).astype(BF)]
    broadcast_in_dim x1 -> x0, other arithmetic: 2.3 us -> none  [body(): grad_hidden = (dcol / smooth_cols)[None]]
where the time goes in v2:
time: 124 us
  Pallas kernels  123 us (99%)
    pallas_call x1, Pallas kernels, main_call(): pl.pallas_call(main_kernel, name='main', out_shape=tuple((jax.ShapeDtypeS...  121 us
    pallas_call x1, Pallas kernels, finish(): pl.pallas_call(finish_kernel, name='finish', out_shape=tuple((jax.ShapeDt...  2.66 us

profile of v2, /device:TPU:1, one launch (start us, length us, event | category | flops | bytes accessed | tf_op | source)
XLA Modules:
  0.0 124.0 jit_solution(15838414625943964804)
XLA Ops:
  0.6 120.7 %main.1 = (f32[128,2048]{1,0:T(8,128)}, f32[128,1024]{1,0:T(8,128)}, f32[512,128]{1,0:T(8,128)}, f32[512,128]{1,0:T(8,128)}, f32[4,128]{1,0:T(4,128)}, /*index=5*/f32[4,128]{1,0:T(4,128)}, f32[64,128]{1,0:T(8,128)}) custom-call(bf16[128,8192]{1,0:T(8,128)(2,1)} %bitcast.7, s32[1,128]{1,0:T(1,128)} %pos_h.1, bf16[128,1024]{1,0:T(8,128)(2,1)} %bitcast.8, ...), custom_call_target="tpu_custom_call" | custom-call | tf_op jit(solution)/shard_map/main/pallas_call | solution.py:718
  121.3 2.7 %finish.1 = (f32[128,2048]{1,0:T(8,128)}, f32[128,1024]{1,0:T(8,128)}, f32[512,128]{1,0:T(8,128)}, f32[512,128]{1,0:T(8,128)}, f32[4,128]{1,0:T(4,128)}, /*index=5*/f32[4,128]{1,0:T(4,128)}, f32[64,128]{1,0:T(8,128)}) custom-call(f32[128,2048]{1,0:T(8,128)} %get-tuple-element.21.refs_0_, f32[128,1024]{1,0:T(8,128)} %get-tuple-element.22.refs_1_, ...), custom_call_target="tpu_custom_call" | custom-call | tf_op jit(solution)/shard_map/finish/pallas_call | solution.py:749

commit v3 on v2

--- a/solution.py
+++ b/solution.py
@@ -39,8 +39,10 @@
         z = lax.rem(self.z + (d + 8), 8)
         return {"ctx": self.x * 4 + lax.rem(z, 4), "dp": lax.div(z, 4) * 2 + self.c}
 
-    def zat(self, z):
-        return {"ctx": self.x * 4 + lax.rem(z, 4), "dp": lax.div(z, 4) * 2 + self.c}
+    def at(self, dx, k):
+        return {
+            "ctx": lax.rem(self.x + (dx + 4), 4) * 4 + lax.rem(self.zl + k, 4), "dp": self.dp
+        }
 
     def zline(self, d):
         return {"ctx": self.x * 4 + lax.rem(self.zl + d, 4), "dp": self.dp}
@@ -112,14 +114,14 @@
     gh_o, gq_o, gkw_o, gvw_o, gks_o, gvs_o, gsm_o,
     hid, pos, queries, kw, vw, ks, vs, smooth, dout, freq,
     cos, sin, inv, ss, st, cb,
-    wbuf, sm, smt, acc, kv,
+    wbuf, sm, smt, smf, acc, kv, gall,
     qr, qt, do, dot_t, scr, dpr, dq, stm, stl, stu,
     a_st, a_rb, a_t, a_zs, a_z,
-    hs, hr, ms, r1, r2, sx, tz, zs, zr, fb,
-    y_s, y_r1, y_r2, yv, gs,
+    wg, hs, hr, fs, fr, fb,
+    y_s, y_r1, y_r2, yv, vp, gs,
     dcol, gq, gkw, gvw, gks, gvs, gsm,
-    ssem, csem, osem, nsem, sibsem, kvsem, asem, asend, azsem, hsem, r1sem, r2sem,
-    zsem, fsem, y1sem, y2sem, vsem, gxsem, gzsem, gssem,
+    ssem, csem, osem, nsem, sibsem, kvsem, gsem, tsem, tysem, asem, asend, azsem,
+    fsem, y1sem, y2sem, vsem, vpsem, gxsem, gzsem,
 ):
     p = Place()
     c = p.c
@@ -131,8 +133,8 @@
     for load in loads:
         load.start()
     xr, xl, yr, yl, sib = p.xn(1), p.xn(-1), p.yn(1), p.yn(-1), p.sib()
-    peers = [xr, xl, p.xn(2), yr, yl, p.yn(2), sib, p.far(1)]
-    peers += [p.zn(k) for k in range(1, 8)]
+    peers = [yr, yl, p.yn(2), sib, p.zn(1), p.zn(-1), p.zn(2), p.zn(-2), p.far(0)]
+    peers += [p.at(dx, k) for dx in range(4) for k in range(4) if dx or k]
     barrier = pltpu.get_barrier_semaphore()
     for peer in peers:
         pl.semaphore_signal(barrier, inc=1, device_id=peer, device_id_type=MESH)
@@ -149,14 +151,15 @@
     own = slot(0, 0)
     for load in loads[:5]:
         load.wait()
-    for q in range(4):
-        rows = slice(q * 128, (q + 1) * 128)
+
+    def quantize(q):
+        rows = pl.ds(pl.multiple_of(q * 128, 128), 128)
         s_row = smooth[:, pl.ds(pl.multiple_of(p.ctx * 512 + q * 128, 128), 128)]
         s_col = spread(s_row)
         for half, (w_ref, step_ref) in enumerate(((kw, ks), (vw, vs))):
             cols = slice(half * HD, (half + 1) * HD)
             weight = w_ref[rows, :].astype(F32)
-            step = step_ref[q : q + 1, :]
+            step = step_ref[pl.ds(q, 1), :]
             ratio = weight * s_col / step
             sine, cosine = sin_cos_turns(ratio)
             sine = sine * (1.0 / TWO_PI)
@@ -166,6 +169,9 @@
             ss[rows, cols] = slope * s_col
             st[rows, cols] = ratio * cosine - sine
             cb[rows, cols] = slope * weight - quant.astype(F32) / s_col
+
+    quantize(c * 2)
+    quantize(c * 2 + 1)
     pl.semaphore_wait(barrier, len(peers))
 
     an = {d: p.mix(p.xn(d), p.zn(d), c) for d in (1, -1)}
@@ -202,17 +208,8 @@
             cols = slice(j * 256, (j + 1) * 256)
             block = hid[:, cols].astype(F32) * inv[:, cols]
             sm[j] = block.astype(BF)
-            smt[j] = block.T.astype(BF)
 
     inv[...] = 1.0 / smooth[...]
-    for load in loads[5:7]:
-        load.wait()
-    angle = spread(pos[...].astype(F32)) * freq[...]
-    cos[...] = jnp.cos(angle)
-    turned = jnp.sin(angle)
-    lane = lax.broadcasted_iota(jnp.int32, (128, 128), 1)
-    sin[...] = jnp.where(lane < HD // 2, -turned, turned)
-
     left, right, far = slot(-1, 0), slot(1, 0), slot(2, 0)
     got(left, 0)
     net(left, 0, an[1])
@@ -221,13 +218,15 @@
     for s, sub in ((left, 0), (right, 1)):
         net(s, sub, bn[1])
         net(s, sub, bn[-1])
-    loads[7].wait()
-    prepare(0, 8)
+    quantize((1 - c) * 2)
+    quantize((1 - c) * 2 + 1)
     for s, sub in ((left, 1), (right, 0)):
         got(s, sub)
         net(s, sub, bn[1])
         net(s, sub, bn[-1])
         to_sib(s)
+    loads[7].wait()
+    prepare(0, 6)
 
     def across(a):
         bl, br = slot(a, -1), slot(a, 1)
@@ -248,57 +247,17 @@
         net(far, sub, bn[-1])
     to_sib(far)
     ready.append(far)
-    prepare(8, 20)
+    prepare(6, 24)
+    for load in loads[5:7]:
+        load.wait()
+    angle = spread(pos[...].astype(F32)) * freq[...]
+    cos[...] = jnp.cos(angle)
+    turned = jnp.sin(angle)
+    lane = lax.broadcasted_iota(jnp.int32, (128, 128), 1)
+    sin[...] = jnp.where(lane < HD // 2, -turned, turned)
+
     ready += across(-1)
-    prepare(20, 32)
-    acc[...] = jnp.zeros_like(acc)
-    dot(own, 0)
-    dot(own, 1)
-    ready += across(1)
-    for s in ready[:5]:
-        dot(s, c)
-    ready += across(2)
-    for s in ready[5:]:
-        dot(s, c)
-    for a in (0, -1, 1, 2):
-        s = slot(a, 2)
-        got(s, 0)
-        got(s, 1)
-        to_sib(s)
-        dot(s, c)
-    for a in (-1, 1, 0, 2):
-        for b in (0, -1, 1, 2):
-            if a == 0 and b == 0:
-                continue
-            s = slot(b, a)
-            from_sib(s)
-            dot(s, 1 - c)
-
-    key_raw = acc[:, :HD]
-    rotated = key_raw * cos[...] + pltpu.roll(key_raw, HD // 2, 1) * sin[...]
-    kv[p.ctx, :, :HD] = rotated.astype(BF)
-    kv[p.ctx, :, HD:] = acc[:, HD:].astype(BF)
-
-    def kslot(d, k):
-        return lax.rem(p.x + (d + 4), 4) * 4 + lax.rem(p.zl + k, 4)
-
-    def ksend(d, k, peer):
-        def what():
-            s = kslot(d, k)
-            return kv.at[s], kv.at[s], kvsem.at[s], peer()
-
-        send(what)
-
-    def kgot(d, k):
-        s = kslot(d, k)
-        arrived(kv.at[s], kvsem.at[s])
-
-    to_right, to_left = (lambda: p.xn(1)), (lambda: p.xn(-1))
-    ksend(0, 0, to_right)
-    ksend(0, 0, to_left)
-    for k in (2, 1, 3):
-        ksend(0, 0, functools.partial(p.zline, k))
-
+    prepare(24, 32)
     groups = qr.shape[0] // 128
     for load in loads[8:]:
         load.wait()
@@ -311,11 +270,88 @@
         d = dout[:, cols]
         do[cols, :] = d
         dot_t[:, cols] = d.astype(F32).T.astype(BF)
+    acc[...] = jnp.zeros_like(acc)
+    dot(own, 0)
+    dot(own, 1)
+    ready += across(1)
+
+    for s in ready[:5]:
+        dot(s, c)
+    ready += across(2)
+    for s in ready[5:]:
+        dot(s, c)
+    for a in (-1, 1, 0, 2):
+        for b in (0, -1, 1):
+            if a == 0 and b == 0:
+                continue
+            s = slot(b, a)
+            from_sib(s)
+            dot(s, 1 - c)
+    for a in (0, -1, 1, 2):
+        s = slot(a, 2)
+        got(s, 0)
+        got(s, 1)
+        to_sib(s)
+        dot(s, c)
+    for a in (-1, 1, 0, 2):
+        s = slot(2, a)
+        from_sib(s)
+        dot(s, 1 - c)
+
+    key_raw = acc[:, :HD]
+    rotated = key_raw * cos[...] + pltpu.roll(key_raw, HD // 2, 1) * sin[...]
+    kv[p.ctx, :, :HD] = rotated.astype(BF)
+    kv[p.ctx, :, HD:] = acc[:, HD:].astype(BF)
+
+    def kslot(d, k):
+        return lax.rem(p.x + (d + 4), 4) * 4 + lax.rem(p.zl + k, 4)
+
+    def ksend(d, k, peer, buf=kv, sem=kvsem):
+        def what():
+            s = kslot(d, k)
+            return buf.at[s], buf.at[s], sem.at[s], peer()
+
+        send(what)
+
+    def kgot(d, k, buf=kv, sem=kvsem):
+        s = kslot(d, k)
+        arrived(buf.at[s], sem.at[s])
+
+    to_right, to_left = (lambda: p.xn(1)), (lambda: p.xn(-1))
+    ksend(0, 0, to_right)
+    ksend(0, 0, to_left)
+    for k in (2, 1, 3):
+        ksend(0, 0, functools.partial(p.zline, k))
+
+    for j in range(32):
+        smt[j * 2 : j * 2 + 2] = sm[j].astype(F32).T.astype(BF).reshape(2, 128, 128)
+    smf[p.y, :, pl.ds(pl.multiple_of(p.ctx * 128, 128), 128)] = smt[p.ctx * 4 + p.y]
     width = 256
     chunks = qr.shape[0] // width
     q_index = p.ctx * 128 + lax.rem(lax.broadcasted_iota(jnp.int32, (1, width), 1), 128)
     first = q_index - jnp.concatenate([pos[...]] * (width // 128), axis=1)
     row = lax.broadcasted_iota(jnp.int32, (256, width), 0)
+    def token_send(dx, k):
+        def what():
+            dest = lax.rem(p.x + dx, 4) * 4 + lax.rem(p.zl + k, 4)
+            cols = pl.ds(pl.multiple_of(p.ctx * 128, 128), 128)
+            return smt.at[dest * 4 + p.y], smf.at[p.y, :, cols], tsem.at[p.ctx], p.at(dx, k)
+
+        send(what)
+
+    def fhalf(d, h):
+        return smf.at[lax.rem(p.y + (d + 4), 4), h * 64 : h * 64 + 64]
+
+    def fsend(d, h, peer):
+        send(
+            lambda: (
+                fhalf(d, h), fhalf(d, h), tysem.at[lax.rem(p.y + (d + 4), 4), h], peer
+            )
+        )
+
+    def fgot(d, h):
+        arrived(fhalf(d, h), tysem.at[lax.rem(p.y + (d + 4), 4), h])
+
     stm[...] = jnp.full_like(stm, -1e30)
     stl[...] = jnp.zeros_like(stl)
     stu[...] = jnp.zeros_like(stu)
@@ -357,6 +393,10 @@
                 kgot(1, k)
                 if k in (1, 3):
                     ksend(1, k, to_left)
+            for dx in range(4):
+                for k in range(4):
+                    if dx or k:
+                        token_send(dx, k)
 
         @pl.when(g == 3)
         def _():
@@ -428,6 +468,18 @@
         @pl.when(j * 2 > p.ctx)
         def _():
             a_st[t] = jnp.zeros((2, 128, 2 * HD), BF)
+
+        @pl.when(t == 4)
+        def _():
+            for dx in range(4):
+                for k in range(4):
+                    if dx or k:
+                        source = kslot(dx, k)
+                        cols = pl.ds(pl.multiple_of(source * 128, 128), 128)
+                        arrived(smf.at[p.y, :, cols], tsem.at[source])
+            for h in (0, 1):
+                fsend(0, h, yr)
+                fsend(0, 1 - h, yl)
 
         @pl.when(q == 2)
         def _():
@@ -472,80 +524,18 @@
     dk = dk * cos[...] - pltpu.roll(dk, HD // 2, 1) * sin[...]
     g = jnp.concatenate([dk, d_kv[:, HD:]], axis=1).astype(BF)
 
-    dirs = (2, 1, -1, 0)
-
-    def wgrad(k):
-        blk = lax.rem(p.x + (dirs[k] + 4), 4)
-        for zl in range(4):
-            j = (blk * 4 + zl) * 2
-            his = jnp.dot(smt[j + (1 - c)], g, preferred_element_type=F32).astype(BF)
-            mine = jnp.dot(smt[j + c], g, preferred_element_type=F32).astype(BF)
-            for u in (0, 1):
-                hs[u, k, zl] = his[u * 128 : u * 128 + 128]
-                ms[u, k, zl] = mine[u * 128 : u * 128 + 128]
-
-    def hsend(u, k):
-        send(lambda: (hs.at[u, k], hr.at[u, k], hsem.at[u, k], sib))
-
-    def hgot(u, k):
-        arrived(hr.at[u, k], hsem.at[u, k])
-
-    def both(u, k, h):
-        part = slice(h * 2, h * 2 + 2)
-        return ms[u, k, part].astype(F32) + hr[u, k, part].astype(F32)
-
-    def xstage(u, k, h, extra=None):
-        value = both(u, k, h)
-        if extra is not None:
-            value = value + extra.astype(F32)
-        sx[u, k, h] = value.astype(BF)
-
-    def xfirst(u):
-        hgot(u, 0)
-        for h in (0, 1):
-            xstage(u, 0, h)
-            peer = (xr, xl)[h]
-            send(
-                functools.partial(
-                    lambda h, peer: (sx.at[u, 0, h], r1.at[u, h], r1sem.at[u, h], peer), h, peer
-                )
-            )
-
-    def xraw(u):
-        hgot(u, 1)
-        xstage(u, 1, 1)
-        send(lambda: (sx.at[u, 1, 1], r2.at[u, 0, 1], r2sem.at[u, 1], xr))
-        hgot(u, 2)
-        xstage(u, 2, 0)
-        send(lambda: (sx.at[u, 2, 0], r2.at[u, 1, 0], r2sem.at[u, 2], xl))
-
-    def xrun(u):
-        arrived(r1.at[u, 0], r1sem.at[u, 0])
-        xstage(u, 1, 0, r1[u, 0])
-        send(lambda: (sx.at[u, 1, 0], r2.at[u, 0, 0], r2sem.at[u, 0], xr))
-        arrived(r1.at[u, 1], r1sem.at[u, 1])
-        xstage(u, 2, 1, r1[u, 1])
-        send(lambda: (sx.at[u, 2, 1], r2.at[u, 1, 1], r2sem.at[u, 3], xl))
-
-    def zsend(u):
-        hgot(u, 3)
-        for i, (s, h) in ((1, (0, 1)), (2, (1, 0)), (0, (0, 0)), (3, (1, 1))):
-            arrived(r2.at[u, s, h], r2sem.at[u, i])
-        for h in (0, 1):
-            total = both(u, 3, h) + r2[u, 0, h].astype(F32) + r2[u, 1, h].astype(F32)
-            tz[u, h * 2 : h * 2 + 2] = total
-            zs[u, h * 2 : h * 2 + 2] = total.astype(BF)
-
-        def what(k):
-            zl = lax.rem(p.zl + k, 4)
-            return zs.at[u, zl], zr.at[p.z], zsem.at[p.z], p.zat(u * 4 + zl)
-
-        for k in (2, 1, 3):
-            send(functools.partial(what, k))
-
-        @pl.when(p.zh != u)
-        def _():
-            Sender.make(send, 60 + u, lambda: what(0)).start()
+    gall[p.ctx] = g
+
+    def gsend(d, k, peer):
+        ksend(d, k, peer, gall, gsem)
+
+    def ggot(d, k):
+        kgot(d, k, gall, gsem)
+
+    gsend(0, 0, to_right)
+    gsend(0, 0, to_left)
+    for k in (2, 1, 3):
+        gsend(0, 0, functools.partial(p.zline, k))
 
     def dgrad(d, h):
         blk = lax.rem(p.y + (d + 4), 4) * 16 + h * 8
@@ -564,58 +554,116 @@
                 piece = piece + extra[:, cols].astype(F32)
             y_s[k, h, :, cols] = piece.astype(BF)
 
-    for k in range(4):
-        wgrad(k)
-        hsend(0, k)
-    for k in range(4):
-        hsend(1, k)
-    xfirst(0)
-    xraw(0)
+    fgot(-1, 0)
+    fsend(-1, 0, yr)
+    fgot(1, 1)
+    fsend(1, 1, yl)
+
     dstore(0, 2, 0)
     send(lambda: (y_s.at[0, 0], y_r1.at[0], y1sem.at[0], yr))
-    xrun(0)
-    xfirst(1)
-    xraw(1)
+    for k in (1, 3, 2):
+        ggot(0, k)
+        gsend(0, k, to_right)
+        gsend(0, k, to_left)
+    ggot(-1, 0)
+    gsend(-1, 0, to_right)
+    ggot(1, 1)
+    gsend(1, 1, to_left)
     dstore(0, 2, 1)
     send(lambda: (y_s.at[0, 1], y_r1.at[1], y1sem.at[1], yl))
+    ggot(-1, 2)
+    gsend(-1, 2, to_right)
+    ggot(1, 3)
+    gsend(1, 3, to_left)
     dstore(1, 1, 1)
     send(lambda: (y_s.at[1, 1], y_r2.at[0, 1], y2sem.at[1], yr))
     dstore(2, -1, 0)
     send(lambda: (y_s.at[2, 0], y_r2.at[1, 0], y2sem.at[2], yl))
-    xrun(1)
+    for k in (1, 3):
+        ggot(-1, k)
+    for k in (0, 2):
+        ggot(1, k)
+    for k in (0, 1, 3, 2):
+        ggot(2, k)
+    for d, h in ((-1, 1), (1, 0), (2, 0), (2, 1)):
+        fgot(d, h)
+
+    g_tokens = gall[...].reshape(2048, 256)
+
+    def wgrad(q):
+        return jnp.dot(smf[q], g_tokens, preferred_element_type=F32)
+
+    for i in (0, 1):
+        q = (1 - c) * 2 + i
+        rows = pl.ds(pl.multiple_of(q * 128, 128), 128)
+        value = wgrad(q)
+        hs[i] = value.astype(BF)
+        wg[rows, :] = value
+    send(lambda: (hs, hr, fsem.at[0], sib))
+    for i in (0, 1):
+        q = c * 2 + i
+        rows = pl.ds(pl.multiple_of(q * 128, 128), 128)
+        wg[rows, :] = wgrad(q)
+    vec = []
+    for q in range(4):
+        rows = slice(q * 128, (q + 1) * 128)
+        t = wg[rows, :] * cb[rows, :]
+        t = t[:, :HD] + t[:, HD:]
+        vec.append(jnp.sum(t.T, axis=0, keepdims=True))
+    yv[p.y] = jnp.concatenate(vec + vec, axis=0)
+    for k in (2, 1, 3):
+        send(functools.partial(lambda k: (yv.at[p.y], yv.at[p.y], vsem.at[k - 1], p.yn(k)), k))
+    arrived(hr, fsem.at[0])
+    for i in (0, 1):
+        rows = pl.ds(pl.multiple_of((c * 2 + i) * 128, 128), 128)
+        fs[i] = (wg[rows, :] + hr[i].astype(F32)).astype(BF)
+    far_id = p.far(0)
+    send(lambda: (fs, fr, fsem.at[1], far_id))
+
+    for k in (1, 3, 2):
+        arrived(yv.at[lax.rem(p.y + (4 - k), 4)], vsem.at[k - 1])
+    vp[0] = (yv[0] + yv[1]) + (yv[2] + yv[3])
+    send(lambda: (vp.at[0], vp.at[1], vpsem.at[0], sib))
+    arrived(vp.at[1], vpsem.at[0])
+    vp[2] = vp[0] + vp[1]
+    send(lambda: (vp.at[2], vp.at[3], vpsem.at[1], far_id))
+
     arrived(y_r1.at[0], y1sem.at[0])
     dstore(1, 1, 0, y_r1.at[0])
     send(lambda: (y_s.at[1, 0], y_r2.at[0, 0], y2sem.at[0], yr))
-    zsend(0)
     arrived(y_r1.at[1], y1sem.at[1])
     dstore(2, -1, 1, y_r1.at[1])
     send(lambda: (y_s.at[2, 1], y_r2.at[1, 1], y2sem.at[3], yl))
+
+    arrived(vp.at[3], vpsem.at[1])
+    own_v = p.zl * 4 + p.x
+    gs[own_v] = vp[2] + vp[3]
+    for k in (2, 1, 3):
+        send(
+            functools.partial(
+                lambda k: (gs.at[own_v], gs.at[own_v], gxsem.at[k - 1], p.xn(k)), k
+            )
+        )
+    arrived(fr, fsem.at[1])
+    fb[pl.ds(c * 2, 2)] = (fs[...].astype(F32) + fr[...].astype(F32)).astype(BF)
+    send(lambda: (fb.at[pl.ds(c * 2, 2)], fb.at[pl.ds(c * 2, 2)], fsem.at[2], sib))
+    for k in (1, 3, 2):
+        arrived(gs.at[p.zl * 4 + lax.rem(p.x + (4 - k), 4)], gxsem.at[k - 1])
+    for i, k in enumerate((2, 1, -1)):
+        send(
+            functools.partial(
+                lambda i, k: (
+                    gs.at[pl.ds(p.zl * 4, 4)], gs.at[pl.ds(p.zl * 4, 4)], gzsem.at[i], p.zn(k)
+                ),
+                i, k,
+            )
+        )
+    inv_cols = inv[:, pl.ds(pl.multiple_of(p.y * 2048, 2048), 2048)]
     for h in (0, 1):
         for i, piece in enumerate(dgrad(0, h)):
             dcol[:, h * 1024 + i * 256 : h * 1024 + (i + 1) * 256] = piece
-    zsend(1)
-
-    mine = c * 2 + p.zh
-    f = tz[p.zh, p.zl]
-    for k in (1, 7, 2, 6, 3, 5, 4):
-        z = lax.rem(p.z + k, 8)
-        arrived(zr.at[z], zsem.at[z])
-        f += zr[z].astype(F32)
-    fb[mine] = f.astype(BF)
-    for i, peer in ((0, p.far(0)), (1, p.far(1)), (2, sib)):
-        send(
-            functools.partial(lambda i, peer: (fb.at[mine], fb.at[mine], fsem.at[i], peer), i, peer)
-        )
-
-    t = f * cb[pl.ds(pl.multiple_of(mine * 128, 128), 128), :]
-    t = t[:, :HD] + t[:, HD:]
-    yv[p.y] = jnp.broadcast_to(jnp.sum(t.T, axis=0, keepdims=True), (8, 128))
-    for k in (2, 1, 3):
-        send(functools.partial(lambda k: (yv.at[p.y], yv.at[p.y], vsem.at[k - 1], p.yn(k)), k))
-
     for i, (s, h) in ((1, (0, 1)), (2, (1, 0)), (0, (0, 0)), (3, (1, 1))):
         arrived(y_r2.at[s, h], y2sem.at[i])
-    inv_cols = inv[:, pl.ds(pl.multiple_of(p.y * 2048, 2048), 2048)]
     for h in (0, 1):
         cols = slice(h * 1024, (h + 1) * 1024)
         total = dcol[:, cols] + y_r2[0, h].astype(F32) + y_r2[1, h].astype(F32)
@@ -623,30 +671,7 @@
     stores.append(pltpu.make_async_copy(dcol, gh_o, osem.at[1]))
     stores[-1].start()
 
-    for k in (1, 3, 2):
-        arrived(yv.at[lax.rem(p.y + (4 - k), 4)], vsem.at[k - 1])
-    gs[c, p.z, p.x] = (yv[0] + yv[1]) + (yv[2] + yv[3])
-    for k in (2, 1, 3):
-        send(
-            functools.partial(
-                lambda k: (
-                    gs.at[c, p.z, p.x], gs.at[c, p.z, p.x], gxsem.at[k - 1], p.xn(k)
-                ),
-                k,
-            )
-        )
-    for k in (1, 3, 2):
-        arrived(gs.at[c, p.z, lax.rem(p.x + (4 - k), 4)], gxsem.at[k - 1])
-    for k in (4, 3, 5, 2, 6, 1, 7):
-        send(
-            functools.partial(
-                lambda k: (gs.at[c, p.z], gs.at[c, p.z], gzsem.at[k - 1], p.zn(k)), k
-            )
-        )
-
-    arrived(fb.at[(1 - c) * 2 + p.zh], fsem.at[2])
-    arrived(fb.at[c * 2 + (1 - p.zh)], fsem.at[0])
-    arrived(fb.at[(1 - c) * 2 + (1 - p.zh)], fsem.at[1])
+    arrived(fb.at[pl.ds((1 - c) * 2, 2)], fsem.at[2])
     for q in range(4):
         rows = slice(q * 128, (q + 1) * 128)
         f = fb[q].astype(F32)
@@ -660,26 +685,15 @@
         stores.append(pltpu.make_async_copy(src, dst, osem.at[2 + i]))
         stores[-1].start()
 
-    for k in (1, 7, 2, 6, 3, 5, 4):
-        arrived(gs.at[c, lax.rem(p.z + (8 - k), 8)], gzsem.at[k - 1])
-    send(lambda: (gs.at[c], gs.at[c], gssem.at[0], sib))
-    arrived(gs.at[1 - c], gssem.at[0])
+    for i, k in enumerate((2, 1, -1)):
+        zl = lax.rem(p.zl + (4 - k), 4)
+        arrived(gs.at[pl.ds(zl * 4, 4)], gzsem.at[i])
     for i in range(16):
-        for q in range(4):
-            r = i * 4 + q
-            gsm[r : r + 1, :] = gs[q // 2, (q % 2) * 4 + i % 4, i // 4, :1, :]
+        gsm[i * 4 : i * 4 + 4, :] = gs[(i % 4) * 4 + i // 4, :4, :]
     stores.append(pltpu.make_async_copy(gsm, gsm_o, osem.at[6]))
     stores[-1].start()
 
     send.drain()
-    for u in (0, 1):
-
-        @pl.when(p.zh != u)
-        def _():
-            send.make(
-                60 + u, lambda: (zs.at[u, p.zl], zr.at[p.z], zsem.at[p.z], p.zat(u * 4 + p.zl))
-            ).wait_send()
-
     for t in range(6):
         acopy(t).wait_send()
     for store in stores:
@@ -696,24 +710,22 @@
     scratch += [pltpu.VMEM(*s) for s in (
         ((128, 128), F32), ((128, 128), F32), ((1, 8192), F32),
         ((512, 256), F32), ((512, 256), F32), ((512, 256), F32),
-        ((64, 128, 256), BF), ((32, 128, 256), BF), ((32, 256, 128), BF), ((128, 256), F32),
-        ((16, 128, 256), BF),
+        ((64, 128, 256), BF), ((32, 128, 256), BF), ((64, 128, 128), BF),
+        ((4, 128, 2048), BF), ((128, 256), F32), ((16, 128, 256), BF), ((16, 128, 256), BF),
         ((rows, HD), BF), ((HD, rows), BF), ((rows, HD), BF), ((HD, rows), BF),
         ((8, 256, rows), F32), ((8, 256, rows), F32), ((HD, rows), F32),
         ((1, rows), F32), ((1, rows), F32), ((1, rows), F32),
         ((8, 2, 128, 256), BF), ((6, 2, 128, 256), BF), ((4, 128, 256), F32),
         ((4, 128, 256), BF), ((3, 128, 256), BF),
-        ((2, 4, 4, 128, 256), BF), ((2, 4, 4, 128, 256), BF), ((2, 4, 4, 128, 256), BF),
-        ((2, 2, 2, 128, 256), BF), ((2, 2, 2, 2, 128, 256), BF), ((2, 3, 2, 2, 128, 256), BF),
-        ((2, 4, 128, 256), F32), ((2, 4, 128, 256), BF), ((8, 128, 256), BF),
-        ((4, 128, 256), BF),
+        ((512, 256), F32), ((2, 128, 256), BF), ((2, 128, 256), BF), ((2, 128, 256), BF),
+        ((2, 128, 256), BF), ((4, 128, 256), BF),
         ((3, 2, 128, 1024), BF), ((2, 128, 1024), BF), ((2, 2, 128, 1024), BF),
-        ((4, 8, 128), F32), ((2, 8, 4, 8, 128), F32),
+        ((4, 8, 128), F32), ((4, 8, 128), F32), ((16, 8, 128), F32),
     )]
     scratch += [pltpu.VMEM(*o) for o in outs]
     scratch += [DMA(s) for s in (
-        (128,), (10,), (7,), (32,), (16,), (16,), (6,), (6,), (3,), (2, 4), (2, 2), (2, 4),
-        (8,), (3,), (2,), (4,), (3,), (3,), (7,), (1,),
+        (160,), (10,), (7,), (32,), (16,), (16,), (16,), (16,), (4, 2), (6,), (6,), (3,),
+        (3,), (2,), (4,), (3,), (2,), (3,), (3,),
     )]
     return pl.pallas_call(
         main_kernel,

time: 124 us -> 105 us (0.85)
  Pallas kernels: 123 us -> 104 us
    pallas_call x1, Pallas kernels: 121 us -> 101 us  [main_call(): pl.pallas_call(main_kernel, name='main', out_shape=tuple((jax.ShapeDtypeS...]
where the time goes in v3:
time: 105 us
  Pallas kernels  104 us (99%)
    pallas_call x1, Pallas kernels, main_call(): pl.pallas_call(main_kernel, name='main', out_shape=tuple((jax.ShapeDtypeS...  101 us
    pallas_call x1, Pallas kernels, finish(): pl.pallas_call(finish_kernel, name='finish', out_shape=tuple((jax.ShapeDt...  2.66 us

profile of v3, /device:TPU:1, one launch (start us, length us, event | category | flops | bytes accessed | tf_op | source)
XLA Modules:
  0.0 104.8 jit_solution(4819882041075466052)
XLA Ops:
  0.6 101.4 %main.1 = (f32[128,2048]{1,0:T(8,128)}, f32[128,1024]{1,0:T(8,128)}, f32[512,128]{1,0:T(8,128)}, f32[512,128]{1,0:T(8,128)}, f32[4,128]{1,0:T(4,128)}, /*index=5*/f32[4,128]{1,0:T(4,128)}, f32[64,128]{1,0:T(8,128)}) custom-call(bf16[128,8192]{1,0:T(8,128)(2,1)} %bitcast.7, s32[1,128]{1,0:T(1,128)} %pos_h.1, bf16[128,1024]{1,0:T(8,128)(2,1)} %bitcast.8, ...), custom_call_target="tpu_custom_call" | custom-call | tf_op jit(solution)/shard_map/main/pallas_call | solution.py:730
  102.1 2.7 %finish.1 = (f32[128,2048]{1,0:T(8,128)}, f32[128,1024]{1,0:T(8,128)}, f32[512,128]{1,0:T(8,128)}, f32[512,128]{1,0:T(8,128)}, f32[4,128]{1,0:T(4,128)}, /*index=5*/f32[4,128]{1,0:T(4,128)}, f32[64,128]{1,0:T(8,128)}) custom-call(f32[128,2048]{1,0:T(8,128)} %get-tuple-element.21.refs_0_, f32[128,1024]{1,0:T(8,128)} %get-tuple-element.22.refs_1_, ...), custom_call_target="tpu_custom_call" | custom-call | tf_op jit(solution)/shard_map/finish/pallas_call | solution.py:761

commit v4 on v3

--- a/solution.py
+++ b/solution.py
@@ -19,6 +19,8 @@
 F32 = jnp.float32
 ANY = pl.BlockSpec(memory_space=pl.ANY)
 DMA = pltpu.SemaphoreType.DMA
+ZOFFSETS = (4, 3, -3, 2, -2, 1, -1)
+VPEERS = ((2, 1), (1, 1), (3, 1), (2, 0), (1, 0), (3, 0), (0, 1))
 
 
 class Place:
@@ -32,26 +34,35 @@
         self.c = lax.rem(self.dp, 2)
         self.z = self.zh * 4 + self.zl
 
+        self.X = [self.x] + [lax.rem(self.x + d, 4) for d in (1, 2, 3)]
+        self.L = [self.zl] + [lax.rem(self.zl + d, 4) for d in (1, 2, 3)]
+        self.Y = [self.y] + [lax.rem(self.y + d, 4) for d in (1, 2, 3)]
+        self.Z = {}
+        for d in (1, -1, 2, -2, 3, -3, 4):
+            z = lax.rem(self.z + (d + 8), 8)
+            self.Z[d] = (self.x * 4 + self.L[d % 4], lax.div(z, 4) * 2 + self.c)
+        self.sibling = self.zh * 2 + (1 - self.c)
+
     def xn(self, d):
-        return {"ctx": lax.rem(self.x + (d + 4), 4) * 4 + self.zl, "dp": self.dp}
+        return {"ctx": self.X[d % 4] * 4 + self.zl, "dp": self.dp}
 
     def zn(self, d):
-        z = lax.rem(self.z + (d + 8), 8)
-        return {"ctx": self.x * 4 + lax.rem(z, 4), "dp": lax.div(z, 4) * 2 + self.c}
+        return {"ctx": self.Z[d][0], "dp": self.Z[d][1]}
 
     def at(self, dx, k):
-        return {
-            "ctx": lax.rem(self.x + (dx + 4), 4) * 4 + lax.rem(self.zl + k, 4), "dp": self.dp
-        }
+        return {"ctx": self.X[dx % 4] * 4 + self.L[k % 4], "dp": self.dp}
 
     def zline(self, d):
-        return {"ctx": self.x * 4 + lax.rem(self.zl + d, 4), "dp": self.dp}
+        return {"ctx": self.x * 4 + self.L[d], "dp": self.dp}
 
     def yn(self, d):
-        return {"tensor": lax.rem(self.y + (d + 4), 4)}
+        return {"tensor": self.Y[d % 4]}
+
+    def ys(self, k, other):
+        return {"tensor": self.Y[k], "dp": self.sibling if other else self.dp}
 
     def sib(self):
-        return {"dp": self.zh * 2 + (1 - self.c)}
+        return {"dp": self.sibling}
 
     def far(self, other):
         c = (1 - self.c) if other else self.c
@@ -87,6 +98,7 @@
     def drain(self):
         for index, what in self.sent:
             self.make(index, what).wait_send()
+        self.sent = []
 
 
 def arrived(ref, sem):
@@ -118,10 +130,10 @@
     qr, qt, do, dot_t, scr, dpr, dq, stm, stl, stu,
     a_st, a_rb, a_t, a_zs, a_z,
     wg, hs, hr, fs, fr, fb,
-    y_s, y_r1, y_r2, yv, vp, gs,
+    y_s, y_r1, y_r2, yv, gs,
     dcol, gq, gkw, gvw, gks, gvs, gsm,
     ssem, csem, osem, nsem, sibsem, kvsem, gsem, tsem, tysem, asem, asend, azsem,
-    fsem, y1sem, y2sem, vsem, vpsem, gxsem, gzsem,
+    fsem, y1sem, y2sem, vsem, gxsem, gzsem,
 ):
     p = Place()
     c = p.c
@@ -133,20 +145,21 @@
     for load in loads:
         load.start()
     xr, xl, yr, yl, sib = p.xn(1), p.xn(-1), p.yn(1), p.yn(-1), p.sib()
-    peers = [yr, yl, p.yn(2), sib, p.zn(1), p.zn(-1), p.zn(2), p.zn(-2), p.far(0)]
+    peers = [yr, yl, p.yn(2), sib] + [p.zn(k) for k in (1, -1, 2, -2, 3, -3, 4)]
+    peers += [p.ys(k, 1) for k in (1, 2, 3)]
     peers += [p.at(dx, k) for dx in range(4) for k in range(4) if dx or k]
     barrier = pltpu.get_barrier_semaphore()
     for peer in peers:
         pl.semaphore_signal(barrier, inc=1, device_id=peer, device_id_type=MESH)
     send = Sender(ssem)
 
-    a0 = p.x * (1 - c) + p.zl * c
-    b0 = p.zl * (1 - c) + p.x * c
+    slots = {}
+    for a in range(4):
+        for b in range(4):
+            slots[a, b] = (p.X[a] * 4 + p.L[b]) * (1 - c) + (p.X[b] * 4 + p.L[a]) * c
 
     def slot(a, b):
-        a = lax.rem(a0 + (a + 4), 4)
-        b = lax.rem(b0 + (b + 4), 4)
-        return (a * 4 + b) * (1 - c) + (b * 4 + a) * c
+        return slots[a % 4, b % 4]
 
     own = slot(0, 0)
     for load in loads[:5]:
@@ -304,7 +317,7 @@
     kv[p.ctx, :, HD:] = acc[:, HD:].astype(BF)
 
     def kslot(d, k):
-        return lax.rem(p.x + (d + 4), 4) * 4 + lax.rem(p.zl + k, 4)
+        return p.X[d % 4] * 4 + p.L[k % 4]
 
     def ksend(d, k, peer, buf=kv, sem=kvsem):
         def what():
@@ -333,24 +346,24 @@
     row = lax.broadcasted_iota(jnp.int32, (256, width), 0)
     def token_send(dx, k):
         def what():
-            dest = lax.rem(p.x + dx, 4) * 4 + lax.rem(p.zl + k, 4)
+            dest = p.X[dx] * 4 + p.L[k]
             cols = pl.ds(pl.multiple_of(p.ctx * 128, 128), 128)
             return smt.at[dest * 4 + p.y], smf.at[p.y, :, cols], tsem.at[p.ctx], p.at(dx, k)
 
         send(what)
 
     def fhalf(d, h):
-        return smf.at[lax.rem(p.y + (d + 4), 4), h * 64 : h * 64 + 64]
+        return smf.at[p.Y[d % 4], h * 64 : h * 64 + 64]
 
     def fsend(d, h, peer):
         send(
             lambda: (
-                fhalf(d, h), fhalf(d, h), tysem.at[lax.rem(p.y + (d + 4), 4), h], peer
+                fhalf(d, h), fhalf(d, h), tysem.at[p.Y[d % 4], h], peer
             )
         )
 
     def fgot(d, h):
-        arrived(fhalf(d, h), tysem.at[lax.rem(p.y + (d + 4), 4), h])
+        arrived(fhalf(d, h), tysem.at[p.Y[d % 4], h])
 
     stm[...] = jnp.full_like(stm, -1e30)
     stl[...] = jnp.zeros_like(stl)
@@ -430,13 +443,13 @@
         stu[:, cols] = delta[n]
     dq[...] = jnp.zeros_like(dq)
 
-    def acopy(t):
+    def acopy(v, t):
         peer = p.mix(p.xn(1), p.xn(-1), lax.rem(t, 2))
         return pltpu.make_async_remote_copy(
-            src_ref=a_st.at[t],
-            dst_ref=a_rb.at[t],
-            send_sem=asend.at[t],
-            recv_sem=asem.at[t],
+            src_ref=a_st.at[v, t],
+            dst_ref=a_rb.at[v, t],
+            send_sem=asend.at[v, t],
+            recv_sem=asem.at[v, t],
             device_id=peer,
             device_id_type=MESH,
         )
@@ -462,12 +475,13 @@
                 dv += jnp.dot(prob.astype(BF), do[cols, :], preferred_element_type=F32)
                 dk += jnp.dot(ds, qr[cols, :], preferred_element_type=F32)
                 dq[:, cols] += jnp.dot(kt, ds, preferred_element_type=F32)
-            a_st[t, :, :, :HD] = (dk * SCALE).astype(BF).reshape(2, 128, HD)
-            a_st[t, :, :, HD:] = dv.astype(BF).reshape(2, 128, HD)
+            a_st[0, t] = (dk * SCALE).astype(BF).reshape(2, 128, HD)
+            a_st[1, t] = dv.astype(BF).reshape(2, 128, HD)
 
         @pl.when(j * 2 > p.ctx)
         def _():
-            a_st[t] = jnp.zeros((2, 128, 2 * HD), BF)
+            a_st[0, t] = jnp.zeros((2, 128, HD), BF)
+            a_st[1, t] = jnp.zeros((2, 128, HD), BF)
 
         @pl.when(t == 4)
         def _():
@@ -483,17 +497,39 @@
 
         @pl.when(q == 2)
         def _():
-            arrived(a_rb.at[t - 4], asem.at[t - 4])
-            a_st[t] = (a_st[t].astype(F32) + a_rb[t - 4].astype(F32)).astype(BF)
-
-        @pl.when(t < 6)
+            for v in (0, 1):
+                arrived(a_rb.at[v, t - 4], asem.at[v, t - 4])
+                total = a_st[v, t].astype(F32) + a_rb[v, t - 4].astype(F32)
+                a_st[v, t] = total.astype(BF)
+                acopy(v, t).start()
+
+        @pl.when(t < 4)
         def _():
-            acopy(t).start()
+            acopy(0, t).start()
+            acopy(1, t).start()
 
         return 0
 
     lax.fori_loop(0, 8, grads, 0)
 
+    for v in (0, 1):
+        for t in (2, 3, 4, 5):
+            arrived(a_rb.at[v, t], asem.at[v, t])
+        for h, (near, run) in enumerate(((3, 4), (2, 5))):
+            total = a_st[v, 6 + h].astype(F32) + a_rb[v, near].astype(F32)
+            total = total + a_rb[v, run].astype(F32)
+            a_t[v, h * 2 : h * 2 + 2] = total
+            a_zs[v, h * 2 : h * 2 + 2] = total.astype(BF)
+        for k in (2, 1, 3):
+            send(
+                functools.partial(
+                    lambda v, k: (
+                        a_zs.at[v, p.L[k % 4]], a_z.at[v, k - 1],
+                        azsem.at[v, k - 1], p.zline(k),
+                    ),
+                    v, k,
+                )
+            )
     for g in range(groups):
         cols = slice(g * 128, (g + 1) * 128)
         t = dq[:, cols].T * SCALE
@@ -501,44 +537,29 @@
     stores = [pltpu.make_async_copy(gq, gq_o, osem.at[0])]
     stores[0].start()
 
-    for t in (2, 3, 4, 5):
-        arrived(a_rb.at[t], asem.at[t])
-    for h, (near, run) in enumerate(((3, 4), (2, 5))):
-        total = a_st[6 + h].astype(F32) + a_rb[near].astype(F32) + a_rb[run].astype(F32)
-        a_t[h * 2 : h * 2 + 2] = total
-        a_zs[h * 2 : h * 2 + 2] = total.astype(BF)
-    for k in (2, 1, 3):
-        send(
-            functools.partial(
-                lambda k: (
-                    a_zs.at[lax.rem(p.zl + k, 4)], a_z.at[k - 1], azsem.at[k - 1], p.zline(k)
-                ),
-                k,
-            )
-        )
-    d_kv = a_t[p.zl]
-    for k in (1, 3, 2):
-        arrived(a_z.at[k - 1], azsem.at[k - 1])
-        d_kv += a_z[k - 1].astype(F32)
-    dk = d_kv[:, :HD]
-    dk = dk * cos[...] - pltpu.roll(dk, HD // 2, 1) * sin[...]
-    g = jnp.concatenate([dk, d_kv[:, HD:]], axis=1).astype(BF)
-
-    gall[p.ctx] = g
-
-    def gsend(d, k, peer):
-        ksend(d, k, peer, gall, gsem)
-
-    def ggot(d, k):
-        kgot(d, k, gall, gsem)
-
-    gsend(0, 0, to_right)
-    gsend(0, 0, to_left)
-    for k in (2, 1, 3):
-        gsend(0, 0, functools.partial(p.zline, k))
-
+    def gsend(v, d, k, peer):
+        ksend(d, k, peer, gall.at[v], gsem.at[v])
+
+    def ggot(v, d, k):
+        kgot(d, k, gall.at[v], gsem.at[v])
+
+    parts = []
+    for v in (0, 1):
+        total = a_t[v, p.zl]
+        for k in (1, 3, 2):
+            arrived(a_z.at[v, k - 1], azsem.at[v, k - 1])
+            total += a_z[v, k - 1].astype(F32)
+        if v == 0:
+            total = total * cos[...] - pltpu.roll(total, HD // 2, 1) * sin[...]
+        parts.append(total.astype(BF))
+        gall[v, p.ctx] = parts[v]
+        for k in (2, 1, 3):
+            gsend(v, 0, 0, functools.partial(p.zline, k))
+        gsend(v, 0, 0, to_right)
+        gsend(v, 0, 0, to_left)
+    g = jnp.concatenate(parts, axis=1)
     def dgrad(d, h):
-        blk = lax.rem(p.y + (d + 4), 4) * 16 + h * 8
+        blk = p.Y[d % 4] * 16 + h * 8
         out = []
         for i in range(4):
             wb = wbuf[pl.ds(blk + i * 2, 2)].reshape(256, 256)
@@ -558,75 +579,90 @@
     fsend(-1, 0, yr)
     fgot(1, 1)
     fsend(1, 1, yl)
-
     dstore(0, 2, 0)
     send(lambda: (y_s.at[0, 0], y_r1.at[0], y1sem.at[0], yr))
-    for k in (1, 3, 2):
-        ggot(0, k)
-        gsend(0, k, to_right)
-        gsend(0, k, to_left)
-    ggot(-1, 0)
-    gsend(-1, 0, to_right)
-    ggot(1, 1)
-    gsend(1, 1, to_left)
     dstore(0, 2, 1)
     send(lambda: (y_s.at[0, 1], y_r1.at[1], y1sem.at[1], yl))
-    ggot(-1, 2)
-    gsend(-1, 2, to_right)
-    ggot(1, 3)
-    gsend(1, 3, to_left)
+
+    for v in (0, 1):
+        for k in (1, 3, 2):
+            ggot(v, 0, k)
+            gsend(v, 0, k, to_right)
+            gsend(v, 0, k, to_left)
     dstore(1, 1, 1)
     send(lambda: (y_s.at[1, 1], y_r2.at[0, 1], y2sem.at[1], yr))
-    dstore(2, -1, 0)
-    send(lambda: (y_s.at[2, 0], y_r2.at[1, 0], y2sem.at[2], yl))
-    for k in (1, 3):
-        ggot(-1, k)
-    for k in (0, 2):
-        ggot(1, k)
-    for k in (0, 1, 3, 2):
-        ggot(2, k)
+    for a, b in ((0, 1), (2, 3)):
+        if a == 2:
+            dstore(2, -1, 0)
+            send(lambda: (y_s.at[2, 0], y_r2.at[1, 0], y2sem.at[2], yl))
+        for v in (0, 1):
+            ggot(v, -1, a)
+            gsend(v, -1, a, to_right)
+            ggot(v, 1, b)
+            gsend(v, 1, b, to_left)
     for d, h in ((-1, 1), (1, 0), (2, 0), (2, 1)):
         fgot(d, h)
 
-    g_tokens = gall[...].reshape(2048, 256)
-
-    def wgrad(q):
-        return jnp.dot(smf[q], g_tokens, preferred_element_type=F32)
-
-    for i in (0, 1):
-        q = (1 - c) * 2 + i
-        rows = pl.ds(pl.multiple_of(q * 128, 128), 128)
-        value = wgrad(q)
-        hs[i] = value.astype(BF)
-        wg[rows, :] = value
-    send(lambda: (hs, hr, fsem.at[0], sib))
-    for i in (0, 1):
-        q = c * 2 + i
-        rows = pl.ds(pl.multiple_of(q * 128, 128), 128)
-        wg[rows, :] = wgrad(q)
-    vec = []
-    for q in range(4):
-        rows = slice(q * 128, (q + 1) * 128)
-        t = wg[rows, :] * cb[rows, :]
-        t = t[:, :HD] + t[:, HD:]
-        vec.append(jnp.sum(t.T, axis=0, keepdims=True))
-    yv[p.y] = jnp.concatenate(vec + vec, axis=0)
+    far_id = p.far(0)
+
+    def fcopy(v):
+        send(lambda: (fs.at[v], fr.at[v], fsem.at[v, 1], far_id))
+
+    early = len(send.sent)
+    vec = [jnp.zeros((1, 128), F32) for _ in range(4)]
+    for v in (0, 1):
+        for k in (1, 3):
+            ggot(v, -1, k)
+        for k in (0, 2):
+            ggot(v, 1, k)
+        for k in (0, 1, 3, 2):
+            ggot(v, 2, k)
+        tokens = gall[v].reshape(2048, HD)
+        for half in (1 - c, c):
+            for i in (0, 1):
+                q = half * 2 + i
+                rows = pl.ds(pl.multiple_of(q * 128, 128), 128)
+                value = jnp.dot(smf[q], tokens, preferred_element_type=F32)
+                wg[v, rows, :] = value
+                if half is not c:
+                    hs[v, i] = value.astype(BF)
+            if half is not c:
+                send(functools.partial(lambda v: (hs.at[v], hr.at[v], fsem.at[v, 0], sib), v))
+        cols = slice(v * HD, (v + 1) * HD)
+        for q in range(4):
+            rows = slice(q * 128, (q + 1) * 128)
+            vec[q] += jnp.sum((wg[v, rows, :] * cb[rows, cols]).T, axis=0, keepdims=True)
+        if v == 1:
+            yv[p.y * 2 + p.c] = jnp.concatenate(vec + vec, axis=0)
+            for k, other in VPEERS:
+                send(
+                    functools.partial(
+                        lambda k, other: (
+                            yv.at[p.y * 2 + p.c], yv.at[p.y * 2 + p.c],
+                            vsem.at[k * 2 + other], p.ys(k, other),
+                        ),
+                        k, other,
+                    )
+                )
+        arrived(hr.at[v], fsem.at[v, 0])
+        for i in (0, 1):
+            rows = pl.ds(pl.multiple_of((c * 2 + i) * 128, 128), 128)
+            fs[v, i] = (wg[v, rows, :] + hr[v, i].astype(F32)).astype(BF)
+        fcopy(v)
+
+    late = send.sent[early:]
+    send.sent = send.sent[:early]
+    for k, other in VPEERS:
+        core = c * (1 - other) + (1 - c) * other
+        arrived(yv.at[p.Y[(4 - k) % 4] * 2 + core], vsem.at[k * 2 + other])
+    first_sent, send.sent = send.sent, []
+    gs[p.z, p.x] = ((yv[0] + yv[1]) + (yv[2] + yv[3])) + ((yv[4] + yv[5]) + (yv[6] + yv[7]))
     for k in (2, 1, 3):
-        send(functools.partial(lambda k: (yv.at[p.y], yv.at[p.y], vsem.at[k - 1], p.yn(k)), k))
-    arrived(hr, fsem.at[0])
-    for i in (0, 1):
-        rows = pl.ds(pl.multiple_of((c * 2 + i) * 128, 128), 128)
-        fs[i] = (wg[rows, :] + hr[i].astype(F32)).astype(BF)
-    far_id = p.far(0)
-    send(lambda: (fs, fr, fsem.at[1], far_id))
-
-    for k in (1, 3, 2):
-        arrived(yv.at[lax.rem(p.y + (4 - k), 4)], vsem.at[k - 1])
-    vp[0] = (yv[0] + yv[1]) + (yv[2] + yv[3])
-    send(lambda: (vp.at[0], vp.at[1], vpsem.at[0], sib))
-    arrived(vp.at[1], vpsem.at[0])
-    vp[2] = vp[0] + vp[1]
-    send(lambda: (vp.at[2], vp.at[3], vpsem.at[1], far_id))
+        send(
+            functools.partial(
+                lambda k: (gs.at[p.z, p.x], gs.at[p.z, p.x], gxsem.at[k - 1], p.xn(k)), k
+            )
+        )
 
     arrived(y_r1.at[0], y1sem.at[0])
     dstore(1, 1, 0, y_r1.at[0])
@@ -635,27 +671,29 @@
     dstore(2, -1, 1, y_r1.at[1])
     send(lambda: (y_s.at[2, 1], y_r2.at[1, 1], y2sem.at[3], yl))
 
-    arrived(vp.at[3], vpsem.at[1])
-    own_v = p.zl * 4 + p.x
-    gs[own_v] = vp[2] + vp[3]
-    for k in (2, 1, 3):
+    for k in (1, 3, 2):
+        arrived(gs.at[p.z, p.X[4 - k]], gxsem.at[k - 1])
+    for k in ZOFFSETS:
         send(
             functools.partial(
-                lambda k: (gs.at[own_v], gs.at[own_v], gxsem.at[k - 1], p.xn(k)), k
+                lambda k: (gs.at[p.z], gs.at[p.z], gzsem.at[k + 3], p.zn(k)), k
             )
         )
-    arrived(fr, fsem.at[1])
-    fb[pl.ds(c * 2, 2)] = (fs[...].astype(F32) + fr[...].astype(F32)).astype(BF)
-    send(lambda: (fb.at[pl.ds(c * 2, 2)], fb.at[pl.ds(c * 2, 2)], fsem.at[2], sib))
-    for k in (1, 3, 2):
-        arrived(gs.at[p.zl * 4 + lax.rem(p.x + (4 - k), 4)], gxsem.at[k - 1])
-    for i, k in enumerate((2, 1, -1)):
+    tail, send.sent = send.sent, first_sent
+    send.drain()
+    for v in (0, 1):
+        for t in range(6):
+            acopy(v, t).wait_send()
+    send.sent = late + tail
+    for v in (0, 1):
+        arrived(fr.at[v], fsem.at[v, 1])
+        fb[v, pl.ds(c * 2, 2)] = (fs[v].astype(F32) + fr[v].astype(F32)).astype(BF)
         send(
             functools.partial(
-                lambda i, k: (
-                    gs.at[pl.ds(p.zl * 4, 4)], gs.at[pl.ds(p.zl * 4, 4)], gzsem.at[i], p.zn(k)
+                lambda v: (
+                    fb.at[v, pl.ds(c * 2, 2)], fb.at[v, pl.ds(c * 2, 2)], fsem.at[v, 2], sib
                 ),
-                i, k,
+                v,
             )
         )
     inv_cols = inv[:, pl.ds(pl.multiple_of(p.y * 2048, 2048), 2048)]
@@ -671,31 +709,27 @@
     stores.append(pltpu.make_async_copy(dcol, gh_o, osem.at[1]))
     stores[-1].start()
 
-    arrived(fb.at[pl.ds((1 - c) * 2, 2)], fsem.at[2])
-    for q in range(4):
-        rows = slice(q * 128, (q + 1) * 128)
-        f = fb[q].astype(F32)
-        o = f * ss[rows, :]
-        gkw[rows, :] = o[:, :HD]
-        gvw[rows, :] = o[:, HD:]
-        o = jnp.sum(f * st[rows, :], axis=0, keepdims=True)
-        gks[q : q + 1, :] = o[:, :HD]
-        gvs[q : q + 1, :] = o[:, HD:]
+    for v, (weights, totals) in enumerate(((gkw, gks), (gvw, gvs))):
+        arrived(fb.at[v, pl.ds((1 - c) * 2, 2)], fsem.at[v, 2])
+        cols = slice(v * HD, (v + 1) * HD)
+        for q in range(4):
+            rows = slice(q * 128, (q + 1) * 128)
+            f = fb[v, q].astype(F32)
+            weights[rows, :] = f * ss[rows, cols]
+            totals[q : q + 1, :] = jnp.sum(f * st[rows, cols], axis=0, keepdims=True)
     for i, (src, dst) in enumerate(((gkw, gkw_o), (gvw, gvw_o), (gks, gks_o), (gvs, gvs_o))):
         stores.append(pltpu.make_async_copy(src, dst, osem.at[2 + i]))
         stores[-1].start()
 
-    for i, k in enumerate((2, 1, -1)):
-        zl = lax.rem(p.zl + (4 - k), 4)
-        arrived(gs.at[pl.ds(zl * 4, 4)], gzsem.at[i])
+    for k in ZOFFSETS:
+        arrived(gs.at[lax.rem(p.z + (8 - k), 8)], gzsem.at[k + 3])
     for i in range(16):
-        gsm[i * 4 : i * 4 + 4, :] = gs[(i % 4) * 4 + i // 4, :4, :]
+        zl, x = i % 4, i // 4
+        gsm[i * 4 : i * 4 + 4, :] = gs[zl, x, :4, :] + gs[4 + zl, x, :4, :]
     stores.append(pltpu.make_async_copy(gsm, gsm_o, osem.at[6]))
     stores[-1].start()
 
     send.drain()
-    for t in range(6):
-        acopy(t).wait_send()
     for store in stores:
         store.wait()
 
@@ -711,21 +745,21 @@
         ((128, 128), F32), ((128, 128), F32), ((1, 8192), F32),
         ((512, 256), F32), ((512, 256), F32), ((512, 256), F32),
         ((64, 128, 256), BF), ((32, 128, 256), BF), ((64, 128, 128), BF),
-        ((4, 128, 2048), BF), ((128, 256), F32), ((16, 128, 256), BF), ((16, 128, 256), BF),
+        ((4, 128, 2048), BF), ((128, 256), F32), ((16, 128, 256), BF), ((2, 16, 128, 128), BF),
         ((rows, HD), BF), ((HD, rows), BF), ((rows, HD), BF), ((HD, rows), BF),
         ((8, 256, rows), F32), ((8, 256, rows), F32), ((HD, rows), F32),
         ((1, rows), F32), ((1, rows), F32), ((1, rows), F32),
-        ((8, 2, 128, 256), BF), ((6, 2, 128, 256), BF), ((4, 128, 256), F32),
-        ((4, 128, 256), BF), ((3, 128, 256), BF),
-        ((512, 256), F32), ((2, 128, 256), BF), ((2, 128, 256), BF), ((2, 128, 256), BF),
-        ((2, 128, 256), BF), ((4, 128, 256), BF),
+        ((2, 8, 2, 128, 128), BF), ((2, 6, 2, 128, 128), BF), ((2, 4, 128, 128), F32),
+        ((2, 4, 128, 128), BF), ((2, 3, 128, 128), BF),
+        ((2, 512, 128), F32), ((2, 2, 128, 128), BF), ((2, 2, 128, 128), BF),
+        ((2, 2, 128, 128), BF), ((2, 2, 128, 128), BF), ((2, 4, 128, 128), BF),
         ((3, 2, 128, 1024), BF), ((2, 128, 1024), BF), ((2, 2, 128, 1024), BF),
-        ((4, 8, 128), F32), ((4, 8, 128), F32), ((16, 8, 128), F32),
+        ((8, 8, 128), F32), ((8, 4, 8, 128), F32),
     )]
     scratch += [pltpu.VMEM(*o) for o in outs]
     scratch += [DMA(s) for s in (
-        (160,), (10,), (7,), (32,), (16,), (16,), (16,), (16,), (4, 2), (6,), (6,), (3,),
-        (3,), (2,), (4,), (3,), (2,), (3,), (3,),
+        (192,), (10,), (7,), (32,), (16,), (16,), (2, 16), (16,), (4, 2), (2, 6), (2, 6),
+        (2, 3), (2, 3), (2,), (4,), (8,), (3,), (8,),
     )]
     return pl.pallas_call(
         main_kernel,

time: 105 us -> 99.7 us (0.950)
  Pallas kernels: 104 us -> 98.9 us
    pallas_call x1, Pallas kernels: 101 us -> 96.2 us  [main_call(): pl.pallas_call(main_kernel, name='main', out_shape=tuple((jax.ShapeDtypeS...]
where the time goes in v4:
time: 99.7 us; the launch traced here: 99.5 us
  Pallas kernels  98.9 us (99%)
    pallas_call x1, Pallas kernels, main_call(): pl.pallas_call(main_kernel, name='main', out_shape=tuple((jax.ShapeDtypeS...  96.2 us
    pallas_call x1, Pallas kernels, finish(): pl.pallas_call(finish_kernel, name='finish', out_shape=tuple((jax.ShapeDt...  2.66 us

profile of v4, /device:TPU:1, one launch (start us, length us, event | category | flops | bytes accessed | tf_op | source)
XLA Modules:
  0.0 99.5 jit_solution(5924525700001916394)
XLA Ops:
  0.6 96.2 %main.1 = (f32[128,2048]{1,0:T(8,128)}, f32[128,1024]{1,0:T(8,128)}, f32[512,128]{1,0:T(8,128)}, f32[512,128]{1,0:T(8,128)}, f32[4,128]{1,0:T(4,128)}, /*index=5*/f32[4,128]{1,0:T(4,128)}, f32[64,128]{1,0:T(8,128)}) custom-call(bf16[128,8192]{1,0:T(8,128)(2,1)} %bitcast.7, s32[1,128]{1,0:T(1,128)} %pos_h.1, bf16[128,1024]{1,0:T(8,128)(2,1)} %bitcast.8, ...), custom_call_target="tpu_custom_call" | custom-call | tf_op jit(solution)/shard_map/main/pallas_call | solution.py:764
  96.9 2.7 %finish.1 = (f32[128,2048]{1,0:T(8,128)}, f32[128,1024]{1,0:T(8,128)}, f32[512,128]{1,0:T(8,128)}, f32[512,128]{1,0:T(8,128)}, f32[4,128]{1,0:T(4,128)}, /*index=5*/f32[4,128]{1,0:T(4,128)}, f32[64,128]{1,0:T(8,128)}) custom-call(f32[128,2048]{1,0:T(8,128)} %get-tuple-element.21.refs_0_, f32[128,1024]{1,0:T(8,128)} %get-tuple-element.22.refs_1_, ...), custom_call_target="tpu_custom_call" | custom-call | tf_op jit(solution)/shard_map/finish/pallas_call | solution.py:795

commit v5 on v4

--- a/solution.py
+++ b/solution.py
@@ -592,7 +592,7 @@
     dstore(1, 1, 1)
     send(lambda: (y_s.at[1, 1], y_r2.at[0, 1], y2sem.at[1], yr))
     for a, b in ((0, 1), (2, 3)):
-        if a == 2:
+        if a == 0:
             dstore(2, -1, 0)
             send(lambda: (y_s.at[2, 0], y_r2.at[1, 0], y2sem.at[2], yl))
         for v in (0, 1):
@@ -650,6 +650,13 @@
             fs[v, i] = (wg[v, rows, :] + hr[v, i].astype(F32)).astype(BF)
         fcopy(v)
 
+    arrived(y_r1.at[0], y1sem.at[0])
+    dstore(1, 1, 0, y_r1.at[0])
+    send(lambda: (y_s.at[1, 0], y_r2.at[0, 0], y2sem.at[0], yr))
+    arrived(y_r1.at[1], y1sem.at[1])
+    dstore(2, -1, 1, y_r1.at[1])
+    send(lambda: (y_s.at[2, 1], y_r2.at[1, 1], y2sem.at[3], yl))
+
     late = send.sent[early:]
     send.sent = send.sent[:early]
     for k, other in VPEERS:
@@ -663,13 +670,6 @@
                 lambda k: (gs.at[p.z, p.x], gs.at[p.z, p.x], gxsem.at[k - 1], p.xn(k)), k
             )
         )
-
-    arrived(y_r1.at[0], y1sem.at[0])
-    dstore(1, 1, 0, y_r1.at[0])
-    send(lambda: (y_s.at[1, 0], y_r2.at[0, 0], y2sem.at[0], yr))
-    arrived(y_r1.at[1], y1sem.at[1])
-    dstore(2, -1, 1, y_r1.at[1])
-    send(lambda: (y_s.at[2, 1], y_r2.at[1, 1], y2sem.at[3], yl))
 
     for k in (1, 3, 2):
         arrived(gs.at[p.z, p.X[4 - k]], gxsem.at[k - 1])

time: 99.7 us -> 101 us (1.013)
  Pallas kernels: 98.9 us -> 100 us
    pallas_call x1, Pallas kernels: 96.2 us -> 97.7 us  [main_call(): pl.pallas_call(main_kernel, name='main', out_shape=tuple((jax.ShapeDtypeS...]
where the time goes in v5:
time: 101 us
  Pallas kernels  100 us (99%)
    pallas_call x1, Pallas kernels, main_call(): pl.pallas_call(main_kernel, name='main', out_shape=tuple((jax.ShapeDtypeS...  97.7 us
    pallas_call x1, Pallas kernels, finish(): pl.pallas_call(finish_kernel, name='finish', out_shape=tuple((jax.ShapeDt...  2.66 us

profile of v5, /device:TPU:1, one launch (start us, length us, event | category | flops | bytes accessed | tf_op | source)
XLA Modules:
  0.0 101.0 jit_solution(1450154261958738285)
XLA Ops:
  0.6 97.7 %main.1 = (f32[128,2048]{1,0:T(8,128)}, f32[128,1024]{1,0:T(8,128)}, f32[512,128]{1,0:T(8,128)}, f32[512,128]{1,0:T(8,128)}, f32[4,128]{1,0:T(4,128)}, /*index=5*/f32[4,128]{1,0:T(4,128)}, f32[64,128]{1,0:T(8,128)}) custom-call(bf16[128,8192]{1,0:T(8,128)(2,1)} %bitcast.7, s32[1,128]{1,0:T(1,128)} %pos_h.1, bf16[128,1024]{1,0:T(8,128)(2,1)} %bitcast.8, ...), custom_call_target="tpu_custom_call" | custom-call | tf_op jit(solution)/shard_map/main/pallas_call | solution.py:764
  98.3 2.7 %finish.1 = (f32[128,2048]{1,0:T(8,128)}, f32[128,1024]{1,0:T(8,128)}, f32[512,128]{1,0:T(8,128)}, f32[512,128]{1,0:T(8,128)}, f32[4,128]{1,0:T(4,128)}, /*index=5*/f32[4,128]{1,0:T(4,128)}, f32[64,128]{1,0:T(8,128)}) custom-call(f32[128,2048]{1,0:T(8,128)} %get-tuple-element.21.refs_0_, f32[128,1024]{1,0:T(8,128)} %get-tuple-element.22.refs_1_, ...), custom_call_target="tpu_custom_call" | custom-call | tf_op jit(solution)/shard_map/finish/pallas_call | solution.py:795
